TPU v7x, 32 devices: a whole 2x2x4 slice. The times are simulated.
32 devices in a mesh: wide: 8 (over z, x), narrow: 4 (over y, core).
Axes of the slice: x: 2, y: 2, z: 4, core: 2. Of those that a mesh axis runs over, the one named last changes fastest.
Arguments:
- tensor_slab: float32 [512, 256, 1024], P(None, 'wide', 'narrow'), may hold values from -220 to 220
- start_basis: float32 [512, 64], replicated, may hold values from -6 to 6
Outputs:
- factor_basis: float32 [512, 64], replicated
- core_unfold: float32 [1024, 64, 256], P('narrow', 'wide')
All inputs are finite; a program needn't handle non-finite values.
Results may differ from a plain program's by a relative error of at most 0.0003.
Values sent between devices are 32-bit elements; how exact they have to be, the bound alone decides.
No kernel may reach another device: no remote copies, remote signals or barrier semaphores. Data moves between devices by JAX's collectives and lax.ppermute only.
A program may use at most 64 MiB of HBM per device.

v0:
```python
import jax
import jax.numpy as jnp
from jax import lax
from jax.sharding import PartitionSpec as P

I1 = 512
ITERS = 8


def orthonormal(block, inner):
    lower_factor = jnp.linalg.cholesky(inner)
    return jax.scipy.linalg.solve_triangular(lower_factor, block.T, lower=True).T


def shards(tensor_slab, start_basis):
    highest = lax.Precision.HIGHEST
    unfold = tensor_slab.reshape(I1, -1)
    basis = start_basis
    local_gram = jnp.dot(unfold, unfold.T, precision=highest, preferred_element_type=jnp.float32)
    gram_full = lax.psum(local_gram, ("wide", "narrow"))
    for sweep_index in range(ITERS):
        block = jnp.dot(gram_full, basis, precision=highest)
        basis = orthonormal(block, jnp.dot(block.T, block, precision=highest))
    core_local = jnp.einsum("ir,ijl->lrj", basis, tensor_slab, precision=highest)
    core_unfold = lax.all_to_all(core_local, "wide", split_axis=1, concat_axis=2, tiled=True)
    return (basis, core_unfold)


def solution(mesh):
    placed = (P(None, "wide", "narrow"), P())
    return jax.shard_map(
        shards,
        mesh=mesh,
        in_specs=placed,
        out_specs=(P(), P("narrow", "wide", None)),
        check_vma=False,
    )
```

profile of v0, /device:TPU:8, one launch (start us, length us, event | category | flops | bytes accessed | tf_op | source)
XLA Modules:
  0.0 386.3 jit_solution(2388660463939528650)
XLA Ops:
  7.2 39.8 %fusion.7 = f32[512,512]{1,0:T(8,128)} fusion(f32[512,32,256]{2,1,0:T(8,128)} %param.5), kind=kOutput, calls=%fused_computation.5 | convolution fusion | flops 25769803776 | bytes 17825792 | tf_op jit(solution)/shard_map/dot_general | solution.py:19
  47.0 131.1 %all-reduce.2.cloned.1.call-done = f32[512,512]{1,0:T(8,128)} async-done(((f32[512,512]{1,0:T(8,128)}), f32[512,512]{1,0:T(8,128)}) %all-reduce.2.cloned.1.call-update) | async-done | bytes 1048592 | tf_op jit(solution)/shard_map/psum | solution.py:20
  178.2 2.4 fusion.65
  180.5 0.3 fusion.66
  180.8 0.1 copy.44
  180.9 5.8 %cholesky.134 = f32[64,64]{1,0:T(8,128)S(1)} custom-call(f32[64,64]{1,0:T(8,128)S(1)} %fusion.50), custom_call_target="Cholesky" | custom-call | tf_op jit(solution)/shard_map/jit(cholesky)/cholesky | solution.py:11
  186.7 0.6 compare_reduce_fusion.7
  187.4 0.7 fusion.27
  188.1 4.9 %custom-call.12 = f32[1,64,64]{1,2,0:T(8,128)S(1)} custom-call(f32[1,64,64]{2,1,0:T(8,128)S(1)} %fusion.27), custom_call_target="InvertDiagBlocksLowerTriangular" | custom-call | tf_op jit(solution)/shard_map/jit(_solve_triangular)/triangular_solve | solution.py:12
  192.9 0.3 fusion.25
  193.3 2.4 fusion.67
  195.6 0.3 fusion.68
  196.0 5.8 %cholesky.145 = f32[64,64]{1,0:T(8,128)S(1)} custom-call(f32[64,64]{1,0:T(8,128)S(1)} %fusion.48), custom_call_target="Cholesky" | custom-call | tf_op jit(solution)/shard_map/jit(cholesky)/cholesky | solution.py:11
  201.9 0.6 compare_reduce_fusion.6
  202.5 0.7 fusion.28
  203.2 4.9 %custom-call.13 = f32[1,64,64]{1,2,0:T(8,128)S(1)} custom-call(f32[1,64,64]{2,1,0:T(8,128)S(1)} %fusion.28), custom_call_target="InvertDiagBlocksLowerTriangular" | custom-call | tf_op jit(solution)/shard_map/jit(_solve_triangular)/triangular_solve | solution.py:12
  208.1 0.3 fusion.23
  208.4 2.4 fusion.69
  210.8 0.3 fusion.70
  211.2 5.8 %cholesky.156 = f32[64,64]{1,0:T(8,128)S(1)} custom-call(f32[64,64]{1,0:T(8,128)S(1)} %fusion.46), custom_call_target="Cholesky" | custom-call | tf_op jit(solution)/shard_map/jit(cholesky)/cholesky | solution.py:11
  217.0 0.6 compare_reduce_fusion.5
  217.7 0.7 fusion.29
  218.3 4.9 %custom-call.14 = f32[1,64,64]{1,2,0:T(8,128)S(1)} custom-call(f32[1,64,64]{2,1,0:T(8,128)S(1)} %fusion.29), custom_call_target="InvertDiagBlocksLowerTriangular" | custom-call | tf_op jit(solution)/shard_map/jit(_solve_triangular)/triangular_solve | solution.py:12
  223.2 0.3 fusion.21
  223.6 2.4 fusion.71
  225.9 0.3 fusion.72
  226.3 5.8 %cholesky.167 = f32[64,64]{1,0:T(8,128)S(1)} custom-call(f32[64,64]{1,0:T(8,128)S(1)} %fusion.44), custom_call_target="Cholesky" | custom-call | tf_op jit(solution)/shard_map/jit(cholesky)/cholesky | solution.py:11
  232.2 0.6 compare_reduce_fusion.4
  232.8 0.7 fusion.30
  233.5 4.9 %custom-call.15 = f32[1,64,64]{1,2,0:T(8,128)S(1)} custom-call(f32[1,64,64]{2,1,0:T(8,128)S(1)} %fusion.30), custom_call_target="InvertDiagBlocksLowerTriangular" | custom-call | tf_op jit(solution)/shard_map/jit(_solve_triangular)/triangular_solve | solution.py:12
  238.4 0.3 fusion.19
  238.7 2.8 fusion.73
  241.5 0.3 fusion.74
  241.9 5.8 %cholesky.178 = f32[64,64]{1,0:T(8,128)S(1)} custom-call(f32[64,64]{1,0:T(8,128)S(1)} %fusion.42), custom_call_target="Cholesky" | custom-call | tf_op jit(solution)/shard_map/jit(cholesky)/cholesky | solution.py:11
  247.7 0.6 compare_reduce_fusion.3
  248.4 0.7 fusion.31
  249.0 4.9 %custom-call.16 = f32[1,64,64]{1,2,0:T(8,128)S(1)} custom-call(f32[1,64,64]{2,1,0:T(8,128)S(1)} %fusion.31), custom_call_target="InvertDiagBlocksLowerTriangular" | custom-call | tf_op jit(solution)/shard_map/jit(_solve_triangular)/triangular_solve | solution.py:12
  253.9 0.3 fusion.17
  254.3 2.4 fusion.75
  256.6 0.3 fusion.76
  257.0 5.8 %cholesky.189 = f32[64,64]{1,0:T(8,128)S(1)} custom-call(f32[64,64]{1,0:T(8,128)S(1)} %fusion.40), custom_call_target="Cholesky" | custom-call | tf_op jit(solution)/shard_map/jit(cholesky)/cholesky | solution.py:11
  262.9 0.6 compare_reduce_fusion.2
  263.5 0.7 fusion.32
  264.2 4.9 %custom-call.17 = f32[1,64,64]{1,2,0:T(8,128)S(1)} custom-call(f32[1,64,64]{2,1,0:T(8,128)S(1)} %fusion.32), custom_call_target="InvertDiagBlocksLowerTriangular" | custom-call | tf_op jit(solution)/shard_map/jit(_solve_triangular)/triangular_solve | solution.py:12
  269.1 0.3 fusion.15
  269.4 2.4 fusion.77
  271.8 0.3 fusion.78
  272.1 5.8 %cholesky.200 = f32[64,64]{1,0:T(8,128)S(1)} custom-call(f32[64,64]{1,0:T(8,128)S(1)} %fusion.38), custom_call_target="Cholesky" | custom-call | tf_op jit(solution)/shard_map/jit(cholesky)/cholesky | solution.py:11
  278.0 0.6 compare_reduce_fusion.1
  278.7 0.7 fusion.33
  279.3 4.9 %custom-call.18 = f32[1,64,64]{1,2,0:T(8,128)S(1)} custom-call(f32[1,64,64]{2,1,0:T(8,128)S(1)} %fusion.33), custom_call_target="InvertDiagBlocksLowerTriangular" | custom-call | tf_op jit(solution)/shard_map/jit(_solve_triangular)/triangular_solve | solution.py:12
  284.2 0.3 fusion.13
  284.6 2.4 fusion.79
  286.9 0.3 fusion.80
  287.3 5.8 %cholesky.211 = f32[64,64]{1,0:T(8,128)S(1)} custom-call(f32[64,64]{1,0:T(8,128)S(1)} %fusion.36), custom_call_target="Cholesky" | custom-call | tf_op jit(solution)/shard_map/jit(cholesky)/cholesky | solution.py:11
  293.2 0.6 compare_reduce_fusion
  293.8 0.7 fusion.34
  294.5 4.9 %custom-call.19 = f32[1,64,64]{1,2,0:T(8,128)S(1)} custom-call(f32[1,64,64]{2,1,0:T(8,128)S(1)} %fusion.34), custom_call_target="InvertDiagBlocksLowerTriangular" | custom-call | tf_op jit(solution)/shard_map/jit(_solve_triangular)/triangular_solve | solution.py:12
  299.4 0.3 fusion.11
  299.7 25.8 %fusion.4 = f32[256,64,32]{0,1,2:T(8,128)S(1)} fusion(f32[512,32,256]{2,1,0:T(8,128)} %param.5, f32[64,512]{1,0:T(8,128)S(1)} %fusion.11), kind=kOutput, calls=%fused_computation.4 | convolution fusion | flops 3221225472 | bytes 19005440 | tf_op jit(solution)/shard_map/ir,ijl->lrj/dot_general | solution.py:24
  325.5 1.2 copy.53
  326.7 50.4 %all_to_all.18 = f32[256,64,32]{0,2,1:T(8,128)S(1)} all-to-all(f32[256,64,32]{0,2,1:T(8,128)S(1)} %copy.53), channel_id=1, replica_groups=mesh['wide'=8,'narrow'=4] {'wide'}, dimensions={1} | all-to-all | bytes 4194304 | tf_op jit(solution)/shard_map/all_to_all | solution.py:25
  377.2 0.1 copy.54
  377.3 2.0 copy.55
  (29 shorter events, 0.9 us)
Async XLA Ops:
  7.2 171.0 %copy-start = (f32[512,64]{0,1:T(8,128)S(1)}, f32[512,64]{0,1:T(8,128)}, u32[]{:S(2)}) copy-start(f32[512,64]{0,1:T(8,128)} %param.6) | copy-start | bytes 393220
  7.2 171.0 %all-reduce.2.cloned.1.call-start = ((), (), s32[]{:S(2)}) async-start(), calls=%async_computation.1 | async-start | bytes 2097152 | tf_op jit(solution)/shard_map/psum | solution.py:20
  299.7 79.6 %copy-start.1 = (f32[64,512]{1,0:T(8,128)}, f32[64,512]{1,0:T(8,128)S(1)}, u32[]{:S(2)}) copy-start(f32[64,512]{1,0:T(8,128)S(1)} %fusion.11) | copy-start | bytes 393220
Sparse Core Ops, SparseCore 0:
  47.2 130.9 all-reduce.1
where the time goes:
time: 392 us; the launch traced here: 386 us
  waiting for transfers between devices  131 us (33%)
  other arithmetic  96.6 us (25%)
  matrix products  89.6 us (23%)
  blocking collectives  50.4 us (13%)
  between operations  14.6 us (4%)
  local copies, waits for them, and re-layouts  3.93 us (1%)
    psum x1, waiting for transfers between devices, shards(): gram_full = lax.psum(local_gram, ('wide', 'narrow'))  131 us
    another operation x24, other arithmetic, orthonormal(): lower_factor = jnp.linalg.cholesky(inner)  52.2 us
    all_to_all x1, blocking collectives, shards(): lax.all_to_all(core_local, 'wide', split_axis=1, concat_axis=2, tiled=True)  50.4 us
    another operation x16, other arithmetic, orthonormal(): jax.scipy.linalg.solve_triangular(lower_factor, block.T, lower=True)  44.4 us
    dot_general x1, matrix products, shards(): jnp.dot(unfold, unfold.T, precision=highest, preferred_element_type=jnp.f...  39.8 us
    dot_general x1, matrix products, shards(): jnp.einsum('ir,ijl->lrj', basis, tensor_slab, precision=highest)  25.8 us
    dot_general x8, matrix products, shards(): block = jnp.dot(gram_full, basis, precision=highest)  19.2 us
  transfers between devices with their start and end apart: 1, of which 1 were waited for; matrix products, arithmetic and copies ran while one was open for 0% of the time, Pallas kernels for 0%

commit v1 on v0

v1 whole, which is shorter than its diff:
```python
import functools

import jax
import jax.numpy as jnp
from jax import lax
from jax.experimental import pallas as pl
from jax.experimental.pallas import tpu as pltpu
from jax.sharding import PartitionSpec as P

ITERS = 8
LANES = 128
ROWS = 8
MIB = 2**20
NT = (((1,), (1,)), ((), ()))
NN = (((1,), (0,)), ((), ()))
f32, bf16 = jnp.float32, jnp.bfloat16


def dot(a, b, dims):
    return lax.dot_general(a, b, dims, preferred_element_type=f32)


def dot_full(a, b, dims):
    return lax.dot_general(a, b, dims, precision=lax.Precision.HIGHEST, preferred_element_type=f32)


def two(x):
    high = x.astype(bf16)
    return high, (x - high.astype(f32)).astype(bf16)


def dot_two(a, b, dims):
    (a_high, a_low), (b_high, b_low) = a, b
    return dot(a_high, b_high, dims) + (dot(a_high, b_low, dims) + dot(a_low, b_high, dims))


def upper_blocks(n):
    return [(p, q) for p in range(n // LANES) for q in range(p, n // LANES)]


def split_rows(x_ref, first, count, high, low):
    rows, depth, lanes = x_ref.shape
    flat = x_ref.reshape(rows * depth, lanes)
    for j in range(count):
        a, b = two(flat[pl.ds(first + j, rows, stride=depth), :])
        high[:, j * lanes : (j + 1) * lanes] = a
        low[:, j * lanes : (j + 1) * lanes] = b


def gram_kernel(x_ref, g_ref, high_0, low_0, high_1, low_1, top, cross, bottom, mixed):
    rows, depth, _ = x_ref.shape
    half = rows // 2
    steps = pl.num_programs(0) * pl.num_programs(1)
    step = pl.program_id(0) * pl.num_programs(1) + pl.program_id(1)

    def add(high, low):
        mixed[...] += dot(high[...], low[...], NT)
        top[...] += dot(high[:half], high[:half], NT)
        cross[...] += dot(high[:half], high[half:], NT)
        bottom[...] += dot(high[half:], high[half:], NT)

    @pl.when(step == 0)
    def _():
        for total in (top, cross, bottom, mixed):
            total[...] = jnp.zeros_like(total)
        split_rows(x_ref, 0, depth // 2, high_0, low_0)
        split_rows(x_ref, depth // 2, depth // 2, high_1, low_1)
        add(high_0, low_0)

    @pl.when(step > 0)
    def _():
        add(high_1, low_1)
        split_rows(x_ref, 0, depth // 2, high_0, low_0)
        add(high_0, low_0)
        split_rows(x_ref, depth // 2, depth // 2, high_1, low_1)

    @pl.when(step == steps - 1)
    def _():
        add(high_1, low_1)
        for k, (p, q) in enumerate(upper_blocks(rows)):
            in_half = half // LANES
            total = top if q < in_half else cross if p < in_half else bottom
            a, b = p % in_half * LANES, q % in_half * LANES
            at_p, at_q = slice(p * LANES, (p + 1) * LANES), slice(q * LANES, (q + 1) * LANES)
            g_ref[k * LANES : (k + 1) * LANES] = (
                total[a : a + LANES, b : b + LANES] + mixed[at_p, at_q] + mixed[at_q, at_p].T
            )


def local_gram(slab):
    rows, second, third = slab.shape
    depth = ROWS
    half = rows // 2
    out = (len(upper_blocks(rows)) * LANES, LANES)
    return pl.pallas_call(
        gram_kernel,
        grid=(second // depth, third // LANES),
        in_specs=[pl.BlockSpec((rows, depth, LANES), lambda j, l: (0, j, l))],
        out_specs=pl.BlockSpec(out, lambda j, l: (0, 0)),
        out_shape=jax.ShapeDtypeStruct(out, f32),
        scratch_shapes=[pltpu.VMEM((rows, depth // 2 * LANES), bf16)] * 4
        + [pltpu.VMEM((half, half), f32)] * 3
        + [pltpu.VMEM((rows, rows), f32)],
        compiler_params=pltpu.CompilerParams(vmem_limit_bytes=32 * MIB),
        name="gram",
    )(slab)


def swap(x, axis, size, bit):
    return lax.ppermute(x, axis, [(i, i ^ bit) for i in range(size)])


def keep_half(x, axis, size, bit):
    halves = x.reshape(2, x.shape[0] // 2, *x.shape[1:])
    mine = (lax.axis_index(axis) & bit) // bit
    keep = lax.dynamic_index_in_dim(halves, mine, 0, keepdims=False)
    send = lax.dynamic_index_in_dim(halves, 1 - mine, 0, keepdims=False)
    return keep + swap(send, axis, size, bit)


def join_half(x, axis, size, bit):
    other = swap(x, axis, size, bit)
    mine = (lax.axis_index(axis) & bit) // bit
    return jnp.where(mine == 0, jnp.concatenate([x, other]), jnp.concatenate([other, x]))


def total(x, wide, narrow):
    halving = [("narrow", narrow, 1 << k) for k in range(narrow.bit_length() - 1)] + [("wide", wide, 1)]
    for axis, size, bit in halving:
        x = keep_half(x, axis, size, bit)
    bits = range(2, wide, 2)
    others = {bit: swap(x, "wide", wide, bit) for bit in bits}
    terms = [x] + [others[bit] for bit in bits]
    while len(terms) > 1:
        terms = [terms[i] + terms[i + 1] for i in range(0, len(terms), 2)]
    x = terms[0]
    for axis, size, bit in reversed(halving):
        x = join_half(x, axis, size, bit)
    return x


def row_of(v, j):
    return jnp.broadcast_to(v[j : j + 1, :], v.shape)


def column_of(v, j):
    return jnp.broadcast_to(v[:, j : j + 1], v.shape)


def inverse_factor(inner, exact):
    n = inner.shape[0]
    groups = n // ROWS
    row = lax.broadcasted_iota(jnp.int32, (ROWS, 2 * n), 0)
    unit = lax.broadcasted_iota(jnp.int32, (n, n), 0) == lax.broadcasted_iota(jnp.int32, (n, n), 1)
    both = jnp.concatenate([inner, unit.astype(f32)], axis=1)
    m = [both[ROWS * q : ROWS * (q + 1)] for q in range(groups)]
    out = []
    for p in range(groups):
        column = {(q, j): column_of(m[q], ROWS * p + j) for q in range(p, groups) for j in range(ROWS)}
        pivots = None
        for j in range(ROWS):
            pivot = row_of(column[p, j], j)
            inverse = pltpu.reciprocal(pivot, approx=True)
            if exact:
                inverse = inverse * (2.0 - pivot * inverse)
                inverse = inverse * (2.0 - pivot * inverse)
            pivots = pivot if pivots is None else jnp.where(row >= j, pivot, pivots)
            later = {k: row_of(column[p, k], j) for k in range(j + 1, ROWS)}
            pivot_row = row_of(m[p], j)
            for q in range(p, groups):
                factor = column[q, j] * inverse
                if q == p:
                    factor = jnp.where(row > j, factor, 0.0)
                for k in range(j + 1, ROWS):
                    column[q, k] = column[q, k] - factor * later[k]
                m[q] = m[q] - factor * pivot_row
        scale = lax.rsqrt(pivots)
        if exact:
            scale = scale * (1.5 - 0.5 * pivots * scale * scale)
        out.append(m[p] * scale)
    return jnp.concatenate(out, axis=0)[:, n:]


def iterate_kernel(packed_ref, start_ref, basis_ref, high, low):
    for k, (p, q) in enumerate(upper_blocks(high.shape[0])):
        at_p, at_q = slice(p * LANES, (p + 1) * LANES), slice(q * LANES, (q + 1) * LANES)
        block = packed_ref[k * LANES : (k + 1) * LANES]
        high[at_p, at_q], low[at_p, at_q] = two(block)
        if p != q:
            high[at_q, at_p], low[at_q, at_p] = two(block.T)

    def times_gram(b):
        return dot_two(b, (high[...], low[...]), NN)

    basis_ref[...] = times_gram(two(start_ref[...]))

    def sweep(_, carry):
        block = two(basis_ref[...])
        product = times_gram(block)
        inverse = inverse_factor(dot_two(block, block, NT), False)
        basis_ref[...] = dot_two(two(inverse), two(product), NN)
        return carry

    lax.fori_loop(0, ITERS - 1, sweep, 0)
    block = basis_ref[...]
    inverse = inverse_factor(dot_full(block, block, NT), True)
    basis_ref[...] = dot_full(inverse, block, NN)


def iterate(packed, start):
    rank, n = start.shape
    return pl.pallas_call(
        iterate_kernel,
        in_specs=[pl.BlockSpec(memory_space=pltpu.VMEM)] * 2,
        out_specs=pl.BlockSpec(memory_space=pltpu.VMEM),
        out_shape=jax.ShapeDtypeStruct((rank, n), f32),
        scratch_shapes=[pltpu.VMEM((n, n), bf16)] * 2,
        compiler_params=pltpu.CompilerParams(vmem_limit_bytes=32 * MIB),
        name="iterate",
    )(packed, start)


def core_kernel(basis_ref, x_ref, out_ref):
    rows, depth, lanes = x_ref.shape
    rank = basis_ref.shape[0]
    groups = out_ref.shape[0]
    flat = x_ref.reshape(rows * depth, lanes)
    basis = jnp.concatenate(two(basis_ref[...]), axis=0)
    for j in range(0, depth, 2):
        pair = [two(flat[pl.ds(j + k, rows, stride=depth), :]) for k in range(2)]
        high, low = (jnp.concatenate(half, axis=1) for half in zip(*pair))
        by_high = dot(basis, high, NN)
        total = by_high[:rank] + (by_high[rank:] + dot(basis[:rank], low, NN))
        for k in range(2):
            piece = total[:, k * lanes : (k + 1) * lanes]
            for g in range(groups):
                size = rank // groups
                out_ref[g, 0, j + k] = piece[g * size : (g + 1) * size]


def truncate(basis, slab, groups):
    rows, second, third = slab.shape
    rank = basis.shape[0]
    depth = ROWS
    return pl.pallas_call(
        core_kernel,
        grid=(second // depth, third // LANES),
        in_specs=[
            pl.BlockSpec((rank, rows), lambda j, l: (0, 0)),
            pl.BlockSpec((rows, depth, LANES), lambda j, l: (0, j, l)),
        ],
        out_specs=pl.BlockSpec((groups, 1, depth, rank // groups, LANES), lambda j, l: (0, l, j, 0, 0)),
        out_shape=jax.ShapeDtypeStruct((groups, third // LANES, second, rank // groups, LANES), f32),
        compiler_params=pltpu.CompilerParams(vmem_limit_bytes=32 * MIB),
        name="truncate",
    )(basis, slab)


def turn_kernel(in_ref, out_ref):
    sources, _, second, rank, lanes = in_ref.shape
    flat = in_ref.reshape(sources * second * rank, lanes)
    flat_out = out_ref.reshape(lanes * rank, LANES)
    for r in range(rank):
        flat_out[pl.ds(r, lanes, stride=rank), :] = flat[pl.ds(r, sources * second, stride=rank), :].T


def turn(parts):
    sources, blocks, second, rank, lanes = parts.shape
    step = LANES // second
    return pl.pallas_call(
        turn_kernel,
        grid=(blocks, sources // step),
        in_specs=[pl.BlockSpec((step, 1, second, rank, lanes), lambda l, s: (s, l, 0, 0, 0))],
        out_specs=pl.BlockSpec((lanes, rank, LANES), lambda l, s: (l, 0, s)),
        out_shape=jax.ShapeDtypeStruct((blocks * lanes, rank, sources * second), f32),
        compiler_params=pltpu.CompilerParams(vmem_limit_bytes=32 * MIB),
        name="turn",
    )(parts)


def shards(wide, narrow, tensor_slab, start_basis):
    packed = total(local_gram(tensor_slab), wide, narrow)
    basis = iterate(packed, start_basis.T)
    parts = truncate(basis, tensor_slab, wide)
    parts = lax.all_to_all(parts, "wide", split_axis=0, concat_axis=0, tiled=True)
    return basis.T, turn(parts)


def solution(mesh):
    return jax.shard_map(
        functools.partial(shards, mesh.shape["wide"], mesh.shape["narrow"]),
        mesh=mesh,
        in_specs=(P(None, "wide", "narrow"), P()),
        out_specs=(P(), P("narrow", "wide", None)),
        check_vma=False,
    )
```

time: 392 us -> 148 us (0.38)
  waiting for transfers between devices: 131 us -> 21.8 us
  other arithmetic: 96.6 us -> 0.17 us
  matrix products: 89.6 us -> 0 us
  Pallas kernels: 0 us -> 46.7 us
  between operations: 14.6 us -> 0.78 us
  starting transfers between devices: 0.04 us -> 10.6 us
  local copies, waits for them, and re-layouts: 3.93 us -> 12.5 us
    psum x1 -> x0, waiting for transfers between devices: 131 us -> none  [shards(): gram_full = lax.psum(local_gram, ('wide', 'narrow'))]
    another operation x40 -> x0, other arithmetic: 96.5 us -> none  [the longest x24 52.2 us: orthonormal(): lower_factor = jnp.linalg.cholesky(inner)]
    dot_general x18 -> x0, matrix products: 86.9 us -> none  [the longest x1 39.8 us: shards(): jnp.dot(unfold, unfold.T, precision=highest, preferred_element_type=jnp.f...]
    pallas_call x0 -> x4, Pallas kernels: none -> 46.7 us  [the longest x1 21.8 us: iterate(): pl.pallas_call(iterate_kernel, in_specs=[pl.BlockSpec(memory_space=pltpu....]
    ppermute x0 -> x9, waiting for transfers between devices: none -> 21.8 us  [swap(): return lax.ppermute(x, axis, [(i, i ^ bit) for i in range(size)])]
    ppermute x0 -> x9, starting transfers between devices: none -> 10.6 us  [swap(): return lax.ppermute(x, axis, [(i, i ^ bit) for i in range(size)])]
    unnamed x5 -> x8, local copies, waits for them, and re-layouts: 1.98 us -> 12.4 us
  transfers between devices with their start and end apart: 1 -> 9, of which waited for: 1 -> 8; matrix products, arithmetic and copies ran while one was open for 0% -> 0% of each run, Pallas kernels for 0% -> 0%
where the time goes in v1:
time: 148 us; the launch traced here: 146 us
  blocking collectives  53.3 us (36%)
  Pallas kernels  46.7 us (32%)
  waiting for transfers between devices  21.8 us (15%)
  local copies, waits for them, and re-layouts  12.5 us (8%)
  starting transfers between devices  10.6 us (7%)
    all_to_all x1, blocking collectives, shards(): lax.all_to_all(parts, 'wide', split_axis=0, concat_axis=0, tiled=True)  53.3 us
    pallas_call x1, Pallas kernels, iterate(): pl.pallas_call(iterate_kernel, in_specs=[pl.BlockSpec(memory_space=pltpu....  21.8 us
    ppermute x9, waiting for transfers between devices, swap(): return lax.ppermute(x, axis, [(i, i ^ bit) for i in range(size)])  21.8 us
    pallas_call x1, Pallas kernels, local_gram(): pl.pallas_call(gram_kernel, grid=(second // depth, third // LANES), in_sp...  13.9 us
    unnamed x8, local copies, waits for them, and re-layouts  12.4 us
    ppermute x9, starting transfers between devices, swap(): return lax.ppermute(x, axis, [(i, i ^ bit) for i in range(size)])  10.6 us
    pallas_call x1, Pallas kernels, truncate(): pl.pallas_call(core_kernel, grid=(second // depth, third // LANES), in_sp...  8.65 us
  transfers between devices with their start and end apart: 9, of which 8 were waited for; matrix products, arithmetic and copies ran while one was open for 0% of the time, Pallas kernels for 0%

profile of v1, /device:TPU:8, one launch (start us, length us, event | category | flops | bytes accessed | tf_op | source)
XLA Modules:
  0.0 145.8 jit_solution(8016936542293761240)
XLA Ops:
  0.6 0.0 copy-start
  0.6 5.8 %copy-done = f32[512,32,256]{2,1,0:T(8,128)S(1)} copy-done((f32[512,32,256]{2,1,0:T(8,128)S(1)}, f32[512,32,256]{2,1,0:T(8,128)}, u32[]{:S(2)}) %copy-start) | copy-done | bytes 16777240
  6.4 13.9 %gram.1 = f32[1280,128]{1,0:T(8,128)S(1)} custom-call(f32[512,32,256]{2,1,0:T(8,128)S(1)} %copy-done), custom_call_target="tpu_custom_call" | custom-call | tf_op jit(solution)/shard_map/gram/pallas_call | solution.py:95
  20.3 0.1 collective-permute-start
  20.4 1.6 %collective-permute-done = f32[640,128]{1,0:T(8,128)S(1)} collective-permute-done((f32[640,128]{1,0:T(8,128)S(1)}, f32[640,128]{1,0:T(8,128)S(1)}, u32[]{:S(2)}, u32[]{:S(2)}) %collective-permute-start) | collective-permute-done | bytes 327712 | tf_op jit(solution)/shard_map/ppermute | solution.py:110
  22.1 0.0 copy-start.3
  22.1 1.6 %collective-permute-start.1 = (f32[320,128]{1,0:T(8,128)S(1)}, f32[320,128]{1,0:T(8,128)S(1)}, u32[]{:S(2)}, u32[]{:S(2)}) collective-permute-start(f32[320,128]{1,0:T(8,128)S(1)} %dynamic-slice_bitcast_fusion.1), channel_id=1, source_target_pairs={{0,2},{1,3},{2,0},{3,1},{4,6},{5,7},{6,4},{7,5},{8,10},{9,11},{10,... | collective-permute-start | bytes 491528 | tf_op jit(solution)/shard_map/ppermute | solution.py:110
  23.7 4.7 %collective-permute-done.1 = f32[320,128]{1,0:T(8,128)S(1)} collective-permute-done((f32[320,128]{1,0:T(8,128)S(1)}, f32[320,128]{1,0:T(8,128)S(1)}, u32[]{:S(2)}, u32[]{:S(2)}) %collective-permute-start.1) | collective-permute-done | bytes 163872 | tf_op jit(solution)/shard_map/ppermute | solution.py:110
  28.5 1.6 %collective-permute-start.2 = (f32[160,128]{1,0:T(8,128)S(1)}, f32[160,128]{1,0:T(8,128)S(1)}, u32[]{:S(2)}, u32[]{:S(2)}) collective-permute-start(f32[160,128]{1,0:T(8,128)S(1)} %dynamic-slice_bitcast_fusion.2), channel_id=1, source_target_pairs={{0,4},{4,0},{8,12},{12,8},{16,20},{20,16},{24,28},{28,24},{1,5},{5... | collective-permute-start | bytes 245768 | tf_op jit(solution)/shard_map/ppermute | solution.py:110
  30.0 3.0 %collective-permute-done.2 = f32[160,128]{1,0:T(8,128)S(1)} collective-permute-done((f32[160,128]{1,0:T(8,128)S(1)}, f32[160,128]{1,0:T(8,128)S(1)}, u32[]{:S(2)}, u32[]{:S(2)}) %collective-permute-start.2) | collective-permute-done | bytes 81952 | tf_op jit(solution)/shard_map/ppermute | solution.py:110
  33.0 1.6 %collective-permute-start.5 = (f32[160,128]{1,0:T(8,128)S(1)}, f32[160,128]{1,0:T(8,128)S(1)}, u32[]{:S(2)}, u32[]{:S(2)}) collective-permute-start(f32[160,128]{1,0:T(8,128)S(1)} %bitcast_add_fusion.2), channel_id=1, source_target_pairs={{0,24},{4,28},{8,16},{12,20},{16,8},{20,12},{24,0},{28,4},{1,25},{... | collective-permute-start | bytes 245768 | tf_op jit(solution)/shard_map/ppermute | solution.py:110
  34.6 1.1 collective-permute-start.4
  35.7 1.4 collective-permute-start.3
  37.1 3.2 %collective-permute-done.5 = f32[160,128]{1,0:T(8,128)S(1)} collective-permute-done((f32[160,128]{1,0:T(8,128)S(1)}, f32[160,128]{1,0:T(8,128)S(1)}, u32[]{:S(2)}, u32[]{:S(2)}) %collective-permute-start.5) | collective-permute-done | bytes 81952 | tf_op jit(solution)/shard_map/ppermute | solution.py:110
  40.3 0.0 collective-permute-done.4
  40.3 1.0 collective-permute-done.3
  41.3 1.6 %collective-permute-start.6 = (f32[160,128]{1,0:T(8,128)S(1)}, f32[160,128]{1,0:T(8,128)S(1)}, u32[]{:S(2)}, u32[]{:S(2)}) collective-permute-start(f32[160,128]{1,0:T(8,128)S(1)} %add_add_fusion), channel_id=1, source_target_pairs={{0,4},{4,0},{8,12},{12,8},{16,20},{20,16},{24,28},{28,24},{1,5},{5... | collective-permute-start | bytes 245768 | tf_op jit(solution)/shard_map/ppermute | solution.py:110
  42.9 2.9 %collective-permute-done.6 = f32[160,128]{1,0:T(8,128)S(1)} collective-permute-done((f32[160,128]{1,0:T(8,128)S(1)}, f32[160,128]{1,0:T(8,128)S(1)}, u32[]{:S(2)}, u32[]{:S(2)}) %collective-permute-start.6) | collective-permute-done | bytes 81952 | tf_op jit(solution)/shard_map/ppermute | solution.py:110
  45.8 1.6 %collective-permute-start.7 = (f32[320,128]{1,0:T(8,128)S(1)}, f32[320,128]{1,0:T(8,128)S(1)}, u32[]{:S(2)}, u32[]{:S(2)}) collective-permute-start(f32[320,128]{1,0:T(8,128)S(1)} %maximum_select_fusion.2), channel_id=1, source_target_pairs={{0,2},{1,3},{2,0},{3,1},{4,6},{5,7},{6,4},{7,5},{8,10},{9,11},{10,... | collective-permute-start | bytes 491528 | tf_op jit(solution)/shard_map/ppermute | solution.py:110
  47.4 3.8 %collective-permute-done.7 = f32[320,128]{1,0:T(8,128)S(1)} collective-permute-done((f32[320,128]{1,0:T(8,128)S(1)}, f32[320,128]{1,0:T(8,128)S(1)}, u32[]{:S(2)}, u32[]{:S(2)}) %collective-permute-start.7) | collective-permute-done | bytes 163872 | tf_op jit(solution)/shard_map/ppermute | solution.py:110
  51.3 0.1 collective-permute-start.8
  51.3 1.6 %collective-permute-done.8 = f32[640,128]{1,0:T(8,128)S(1)} collective-permute-done((f32[640,128]{1,0:T(8,128)S(1)}, f32[640,128]{1,0:T(8,128)S(1)}, u32[]{:S(2)}, u32[]{:S(2)}) %collective-permute-start.8) | collective-permute-done | bytes 327712 | tf_op jit(solution)/shard_map/ppermute | solution.py:110
  53.0 0.0 copy-done.3
  53.0 21.8 %iterate.1.basis_ref = f32[64,512]{1,0:T(8,128)} custom-call(f32[1280,128]{1,0:T(8,128)S(1)} %maximum_select_fusion.packed_ref, f32[64,512]{1,0:T(8,128)S(1)} %bitcast.20), custom_call_target="tpu_custom_call" | custom-call | tf_op jit(solution)/shard_map/iterate/pallas_call | solution.py:212
  74.8 0.0 copy-start.1
  74.8 5.8 %copy-done.1 = f32[512,32,256]{2,1,0:T(8,128)S(1)} copy-done((f32[512,32,256]{2,1,0:T(8,128)S(1)}, f32[512,32,256]{2,1,0:T(8,128)}, u32[]{:S(2)}) %copy-start.1) | copy-done | bytes 16777240
  80.6 0.0 copy-start.2
  80.6 0.9 copy-done.2
  81.5 8.7 %truncate.1 = f32[8,2,32,8,128]{4,3,2,1,0:T(8,128)S(1)} custom-call(f32[64,512]{1,0:T(8,128)S(1)} %copy-done.2, f32[512,32,256]{2,1,0:T(8,128)S(1)} %copy-done.1), custom_call_target="tpu_custom_call" | custom-call | tf_op jit(solution)/shard_map/truncate/pallas_call | solution.py:245
  90.2 53.3 %all_to_all.5.in_ref = f32[8,2,32,8,128]{4,3,2,1,0:T(8,128)S(1)} all-to-all(f32[8,2,32,8,128]{4,3,2,1,0:T(8,128)S(1)} %truncate.1), channel_id=1, replica_groups=mesh['wide'=8,'narrow'=4] {'wide'}, dimensions={0} | all-to-all | bytes 4194304 | tf_op jit(solution)/shard_map/all_to_all | solution.py:285
  143.4 2.3 %turn.1 = f32[256,8,256]{2,1,0:T(8,128)} custom-call(f32[8,2,32,8,128]{4,3,2,1,0:T(8,128)S(1)} %all_to_all.5.in_ref), custom_call_target="tpu_custom_call" | custom-call | tf_op jit(solution)/shard_map/turn/pallas_call | solution.py:270
  (10 shorter events, 0.2 us)
Async XLA Ops:
  0.6 5.8 %copy-start = (f32[512,32,256]{2,1,0:T(8,128)S(1)}, f32[512,32,256]{2,1,0:T(8,128)}, u32[]{:S(2)}) copy-start(f32[512,32,256]{2,1,0:T(8,128)} %x_ref.3) | copy-start | bytes 50331652
  20.3 1.7 %collective-permute-start = (f32[640,128]{1,0:T(8,128)S(1)}, f32[640,128]{1,0:T(8,128)S(1)}, u32[]{:S(2)}, u32[]{:S(2)}) collective-permute-start(f32[640,128]{1,0:T(8,128)S(1)} %dynamic-slice_bitcast_fusion), channel_id=1, source_target_pairs={{0,1},{1,0},{2,3},{3,2},{4,5},{5,4},{6,7},{7,6},{8,9},{9,8},{10,11... | collective-permute-start | bytes 983048 | tf_op jit(solution)/shard_map/ppermute | solution.py:110
  22.1 30.9 %copy-start.3 = (f32[512,64]{0,1:T(8,128)S(1)}, f32[512,64]{0,1:T(8,128)}, u32[]{:S(2)}) copy-start(f32[512,64]{0,1:T(8,128)} %param.3) | copy-start | bytes 393220
  22.1 6.3 %collective-permute-start.1 = (f32[320,128]{1,0:T(8,128)S(1)}, f32[320,128]{1,0:T(8,128)S(1)}, u32[]{:S(2)}, u32[]{:S(2)}) collective-permute-start(f32[320,128]{1,0:T(8,128)S(1)} %dynamic-slice_bitcast_fusion.1), channel_id=1, source_target_pairs={{0,2},{1,3},{2,0},{3,1},{4,6},{5,7},{6,4},{7,5},{8,10},{9,11},{10,... | collective-permute-start | bytes 491528 | tf_op jit(solution)/shard_map/ppermute | solution.py:110
  28.5 4.5 %collective-permute-start.2 = (f32[160,128]{1,0:T(8,128)S(1)}, f32[160,128]{1,0:T(8,128)S(1)}, u32[]{:S(2)}, u32[]{:S(2)}) collective-permute-start(f32[160,128]{1,0:T(8,128)S(1)} %dynamic-slice_bitcast_fusion.2), channel_id=1, source_target_pairs={{0,4},{4,0},{8,12},{12,8},{16,20},{20,16},{24,28},{28,24},{1,5},{5... | collective-permute-start | bytes 245768 | tf_op jit(solution)/shard_map/ppermute | solution.py:110
  33.0 7.3 %collective-permute-start.5 = (f32[160,128]{1,0:T(8,128)S(1)}, f32[160,128]{1,0:T(8,128)S(1)}, u32[]{:S(2)}, u32[]{:S(2)}) collective-permute-start(f32[160,128]{1,0:T(8,128)S(1)} %bitcast_add_fusion.2), channel_id=1, source_target_pairs={{0,24},{4,28},{8,16},{12,20},{16,8},{20,12},{24,0},{28,4},{1,25},{... | collective-permute-start | bytes 245768 | tf_op jit(solution)/shard_map/ppermute | solution.py:110
  34.6 5.6 %collective-permute-start.4 = (f32[160,128]{1,0:T(8,128)S(1)}, f32[160,128]{1,0:T(8,128)S(1)}, u32[]{:S(2)}, u32[]{:S(2)}) collective-permute-start(f32[160,128]{1,0:T(8,128)S(1)} %bitcast_add_fusion.2), channel_id=1, source_target_pairs={{0,16},{4,20},{8,24},{12,28},{16,0},{20,4},{24,8},{28,12},{1,17},{... | collective-permute-start | bytes 245768 | tf_op jit(solution)/shard_map/ppermute | solution.py:110
  35.7 5.6 %collective-permute-start.3 = (f32[160,128]{1,0:T(8,128)S(1)}, f32[160,128]{1,0:T(8,128)S(1)}, u32[]{:S(2)}, u32[]{:S(2)}) collective-permute-start(f32[160,128]{1,0:T(8,128)S(1)} %bitcast_add_fusion.2), channel_id=1, source_target_pairs={{0,8},{4,12},{8,0},{12,4},{16,24},{20,28},{24,16},{28,20},{1,9},{5... | collective-permute-start | bytes 245768 | tf_op jit(solution)/shard_map/ppermute | solution.py:110
  41.3 4.5 %collective-permute-start.6 = (f32[160,128]{1,0:T(8,128)S(1)}, f32[160,128]{1,0:T(8,128)S(1)}, u32[]{:S(2)}, u32[]{:S(2)}) collective-permute-start(f32[160,128]{1,0:T(8,128)S(1)} %add_add_fusion), channel_id=1, source_target_pairs={{0,4},{4,0},{8,12},{12,8},{16,20},{20,16},{24,28},{28,24},{1,5},{5... | collective-permute-start | bytes 245768 | tf_op jit(solution)/shard_map/ppermute | solution.py:110
  45.8 5.4 %collective-permute-start.7 = (f32[320,128]{1,0:T(8,128)S(1)}, f32[320,128]{1,0:T(8,128)S(1)}, u32[]{:S(2)}, u32[]{:S(2)}) collective-permute-start(f32[320,128]{1,0:T(8,128)S(1)} %maximum_select_fusion.2), channel_id=1, source_target_pairs={{0,2},{1,3},{2,0},{3,1},{4,6},{5,7},{6,4},{7,5},{8,10},{9,11},{10,... | collective-permute-start | bytes 491528 | tf_op jit(solution)/shard_map/ppermute | solution.py:110
  51.3 1.7 %collective-permute-start.8 = (f32[640,128]{1,0:T(8,128)S(1)}, f32[640,128]{1,0:T(8,128)S(1)}, u32[]{:S(2)}, u32[]{:S(2)}) collective-permute-start(f32[640,128]{1,0:T(8,128)S(1)} %maximum_select_fusion.1), channel_id=1, source_target_pairs={{0,1},{1,0},{2,3},{3,2},{4,5},{5,4},{6,7},{7,6},{8,9},{9,8},{10,11... | collective-permute-start | bytes 983048 | tf_op jit(solution)/shard_map/ppermute | solution.py:110
  74.8 5.8 %copy-start.1 = (f32[512,32,256]{2,1,0:T(8,128)S(1)}, f32[512,32,256]{2,1,0:T(8,128)}, u32[]{:S(2)}) copy-start(f32[512,32,256]{2,1,0:T(8,128)} %x_ref.3) | copy-start | bytes 50331652
  80.6 0.9 copy-start.2

commit v2 on v1

--- a/solution.py
+++ b/solution.py
@@ -10,6 +10,7 @@
 ITERS = 8
 LANES = 128
 ROWS = 8
+DEPTH = 4
 MIB = 2**20
 NT = (((1,), (1,)), ((), ()))
 NN = (((1,), (0,)), ((), ()))
@@ -101,42 +102,51 @@
         scratch_shapes=[pltpu.VMEM((rows, depth // 2 * LANES), bf16)] * 4
         + [pltpu.VMEM((half, half), f32)] * 3
         + [pltpu.VMEM((rows, rows), f32)],
-        compiler_params=pltpu.CompilerParams(vmem_limit_bytes=32 * MIB),
+        compiler_params=pltpu.CompilerParams(vmem_limit_bytes=50 * MIB),
         name="gram",
     )(slab)
 
 
-def swap(x, axis, size, bit):
-    return lax.ppermute(x, axis, [(i, i ^ bit) for i in range(size)])
-
-
-def keep_half(x, axis, size, bit):
-    halves = x.reshape(2, x.shape[0] // 2, *x.shape[1:])
-    mine = (lax.axis_index(axis) & bit) // bit
-    keep = lax.dynamic_index_in_dim(halves, mine, 0, keepdims=False)
-    send = lax.dynamic_index_in_dim(halves, 1 - mine, 0, keepdims=False)
-    return keep + swap(send, axis, size, bit)
-
-
-def join_half(x, axis, size, bit):
-    other = swap(x, axis, size, bit)
-    mine = (lax.axis_index(axis) & bit) // bit
-    return jnp.where(mine == 0, jnp.concatenate([x, other]), jnp.concatenate([other, x]))
+def swap(x, devices, mask):
+    return lax.ppermute(x, ("wide", "narrow"), [(i, i ^ mask) for i in range(devices)])
+
+
+def masks_of(bits):
+    return [sum(bit for i, bit in enumerate(bits) if k >> i & 1) for k in range(1 << len(bits))]
+
+
+def pairwise(terms):
+    while len(terms) > 1:
+        terms = [a + b for a, b in zip(terms[::2], terms[1::2])]
+    return terms[0]
+
+
+def scatter_sum(x, devices, bits):
+    parts = x.reshape(1 << len(bits), -1, x.shape[-1])
+    me = lax.axis_index(("wide", "narrow"))
+    place = sum((me & bit) // bit << i for i, bit in enumerate(bits))
+    terms = [lax.dynamic_index_in_dim(parts, place ^ k, 0, keepdims=False) for k in range(len(parts))]
+    return pairwise(terms[:1] + [swap(t, devices, mask) for t, mask in zip(terms[1:], masks_of(bits)[1:])])
+
+
+def gather(x, devices, bits):
+    me = lax.axis_index(("wide", "narrow"))
+    parts = [x] + [swap(x, devices, mask) for mask in masks_of(bits)[1:]]
+    for i, bit in enumerate(bits):
+        parts = [jnp.where(me & bit == 0, parts[k], parts[k ^ 1 << i]) for k in range(len(parts))]
+    return jnp.concatenate(parts)
 
 
 def total(x, wide, narrow):
-    halving = [("narrow", narrow, 1 << k) for k in range(narrow.bit_length() - 1)] + [("wide", wide, 1)]
-    for axis, size, bit in halving:
-        x = keep_half(x, axis, size, bit)
-    bits = range(2, wide, 2)
-    others = {bit: swap(x, "wide", wide, bit) for bit in bits}
-    terms = [x] + [others[bit] for bit in bits]
-    while len(terms) > 1:
-        terms = [terms[i] + terms[i + 1] for i in range(0, len(terms), 2)]
-    x = terms[0]
-    for axis, size, bit in reversed(halving):
-        x = join_half(x, axis, size, bit)
-    return x
+    devices = wide * narrow
+    core = [1]
+    plane = [1 << k for k in range(1, narrow.bit_length())]
+    line = [narrow << k for k in range(1, wide.bit_length() - 1)]
+    x = scatter_sum(x, devices, core)
+    x = scatter_sum(x, devices, plane)
+    x = pairwise([x] + [swap(x, devices, mask) for mask in masks_of(line)[1:]])
+    x = gather(x, devices, plane)
+    return gather(x, devices, core)
 
 
 def row_of(v, j):
@@ -181,7 +191,19 @@
     return jnp.concatenate(out, axis=0)[:, n:]
 
 
-def iterate_kernel(packed_ref, start_ref, basis_ref, high, low):
+def iterate_kernel(order_ref, packed_ref, start_ref, slab_ref, basis_ref, *rest):
+    *out_refs, high, low, by_group, slab, sems = rest
+    blocks, strips, rows, depth, lanes = slab.shape
+    copies = [
+        pltpu.make_async_copy(
+            slab_ref.at[:, pl.ds(s * depth, depth), pl.ds(l * lanes, lanes)], slab.at[l, s], sems.at[l, s]
+        )
+        for l in range(blocks)
+        for s in range(strips)
+    ]
+    for copy in copies:
+        copy.start()
+
     for k, (p, q) in enumerate(upper_blocks(high.shape[0])):
         at_p, at_q = slice(p * LANES, (p + 1) * LANES), slice(q * LANES, (q + 1) * LANES)
         block = packed_ref[k * LANES : (k + 1) * LANES]
@@ -206,84 +228,124 @@
     inverse = inverse_factor(dot_full(block, block, NT), True)
     basis_ref[...] = dot_full(inverse, block, NN)
 
-
-def iterate(packed, start):
+    rank = basis_ref.shape[0]
+    size = rank // len(out_refs)
+    for g in range(len(out_refs)):
+        by_group[g] = basis_ref[g * size : (g + 1) * size]
+    basis = jnp.concatenate([by_group[order_ref[g]] for g in range(len(out_refs))], axis=0)
+    basis = jnp.concatenate(two(basis), axis=0)
+    flat = slab.reshape(blocks * strips * rows * depth, lanes)
+    for copy in copies:
+        copy.wait()
+
+    def columns(step, carry):
+        for j in range(0, depth, 2):
+            at = step * rows * depth + j
+            pair = [two(flat[pl.ds(at + k, rows, stride=depth), :]) for k in range(2)]
+            high_x, low_x = (jnp.concatenate(half, axis=1) for half in zip(*pair))
+            by_high = dot(basis, high_x, NN)
+            field = by_high[:rank] + (by_high[rank:] + dot(basis[:rank], low_x, NN))
+            for k in range(2):
+                for g, out_ref in enumerate(out_refs):
+                    out_ref[step // strips, step % strips * depth + j + k] = field[
+                        g * size : (g + 1) * size, k * lanes : (k + 1) * lanes
+                    ]
+        return carry
+
+    lax.fori_loop(0, blocks * strips, columns, 0)
+
+
+def iterate(order, packed, start, tensor_slab):
     rank, n = start.shape
+    rows, second, third = tensor_slab.shape
+    groups = order.shape[0]
+    field = jax.ShapeDtypeStruct((third // LANES, second, rank // groups, LANES), f32)
+    vmem = pl.BlockSpec(memory_space=pltpu.VMEM)
     return pl.pallas_call(
         iterate_kernel,
-        in_specs=[pl.BlockSpec(memory_space=pltpu.VMEM)] * 2,
-        out_specs=pl.BlockSpec(memory_space=pltpu.VMEM),
-        out_shape=jax.ShapeDtypeStruct((rank, n), f32),
-        scratch_shapes=[pltpu.VMEM((n, n), bf16)] * 2,
-        compiler_params=pltpu.CompilerParams(vmem_limit_bytes=32 * MIB),
+        in_specs=[pl.BlockSpec(memory_space=pltpu.SMEM), vmem, vmem, pl.BlockSpec(memory_space=pl.ANY)],
+        out_specs=[vmem] * (1 + groups),
+        out_shape=[jax.ShapeDtypeStruct((rank, n), f32)] + [field] * groups,
+        scratch_shapes=[pltpu.VMEM((n, n), bf16)] * 2
+        + [pltpu.VMEM((groups, rank // groups, n), f32)]
+        + [
+            pltpu.VMEM((third // LANES, second // DEPTH, rows, DEPTH, LANES), f32),
+            pltpu.SemaphoreType.DMA((third // LANES, second // DEPTH)),
+        ],
+        compiler_params=pltpu.CompilerParams(vmem_limit_bytes=44 * MIB),
         name="iterate",
-    )(packed, start)
-
-
-def core_kernel(basis_ref, x_ref, out_ref):
-    rows, depth, lanes = x_ref.shape
-    rank = basis_ref.shape[0]
-    groups = out_ref.shape[0]
-    flat = x_ref.reshape(rows * depth, lanes)
-    basis = jnp.concatenate(two(basis_ref[...]), axis=0)
-    for j in range(0, depth, 2):
-        pair = [two(flat[pl.ds(j + k, rows, stride=depth), :]) for k in range(2)]
-        high, low = (jnp.concatenate(half, axis=1) for half in zip(*pair))
-        by_high = dot(basis, high, NN)
-        total = by_high[:rank] + (by_high[rank:] + dot(basis[:rank], low, NN))
-        for k in range(2):
-            piece = total[:, k * lanes : (k + 1) * lanes]
-            for g in range(groups):
-                size = rank // groups
-                out_ref[g, 0, j + k] = piece[g * size : (g + 1) * size]
-
-
-def truncate(basis, slab, groups):
-    rows, second, third = slab.shape
-    rank = basis.shape[0]
-    depth = ROWS
-    return pl.pallas_call(
-        core_kernel,
-        grid=(second // depth, third // LANES),
-        in_specs=[
-            pl.BlockSpec((rank, rows), lambda j, l: (0, 0)),
-            pl.BlockSpec((rows, depth, LANES), lambda j, l: (0, j, l)),
-        ],
-        out_specs=pl.BlockSpec((groups, 1, depth, rank // groups, LANES), lambda j, l: (0, l, j, 0, 0)),
-        out_shape=jax.ShapeDtypeStruct((groups, third // LANES, second, rank // groups, LANES), f32),
-        compiler_params=pltpu.CompilerParams(vmem_limit_bytes=32 * MIB),
-        name="truncate",
-    )(basis, slab)
-
-
-def turn_kernel(in_ref, out_ref):
-    sources, _, second, rank, lanes = in_ref.shape
-    flat = in_ref.reshape(sources * second * rank, lanes)
+    )(order, packed, start, tensor_slab)
+
+
+def exchange(parts, wide, narrow, near):
+    def move(mask, part):
+        return swap(part, wide * narrow, mask * narrow)
+
+    received = {0: parts[0]}
+    early = [*range(wide - 1, near, -1), *range(near - 1, 0, -2)]
+    for mask in early:
+        received[mask] = move(mask, parts[mask])
+    late = [mask for mask in range(near, 0, -1) if mask not in early]
+    *arrived, held = lax.optimization_barrier(
+        (*[received[mask] for mask in range(near - 1, 0, -2)], [parts[mask] for mask in late])
+    )
+    received.update(zip(range(near - 1, 0, -2), arrived))
+    for mask, part in zip(late, held):
+        received[mask] = move(mask, part)
+    return [received[mask] for mask in range(near)], [received[mask] for mask in range(near, wide)]
+
+
+def turn_kernel(tiles_ref, order_ref, *refs):
+    refs = refs[-2 - order_ref.shape[0] :]
+    *in_refs, out_ref, held = refs
+    _, second, rank, lanes = in_refs[0].shape
+    step = LANES // second
+    at = pl.program_id(1)
+
+    @pl.when(at == 0)
+    def _():
+        for s, in_ref in enumerate(in_refs):
+            held[s // step * step + order_ref[s]] = in_ref[0]
+
+    flat = held.reshape(len(in_refs) * second * rank, lanes)
     flat_out = out_ref.reshape(lanes * rank, LANES)
+    first = at * (step * second * rank)
     for r in range(rank):
-        flat_out[pl.ds(r, lanes, stride=rank), :] = flat[pl.ds(r, sources * second, stride=rank), :].T
-
-
-def turn(parts):
-    sources, blocks, second, rank, lanes = parts.shape
-    step = LANES // second
+        rows = flat[pl.ds(first + r, step * second, stride=rank), :]
+        flat_out[pl.ds(r, lanes, stride=rank), :] = rows.T
+
+
+def turn(tiles, order, parts, sources, before=None):
+    blocks, second, rank, lanes = parts[0].shape
+    part = pl.BlockSpec((1, second, rank, lanes), lambda l, s, tiles, order: (l, 0, 0, 0))
+    earlier = [] if before is None else [before]
     return pl.pallas_call(
         turn_kernel,
-        grid=(blocks, sources // step),
-        in_specs=[pl.BlockSpec((step, 1, second, rank, lanes), lambda l, s: (s, l, 0, 0, 0))],
-        out_specs=pl.BlockSpec((lanes, rank, LANES), lambda l, s: (l, 0, s)),
+        grid_spec=pltpu.PrefetchScalarGridSpec(
+            num_scalar_prefetch=2,
+            grid=(blocks, len(parts) * second // LANES),
+            in_specs=[pl.BlockSpec(memory_space=pl.ANY)] * len(earlier) + [part] * len(parts),
+            out_specs=pl.BlockSpec((lanes, rank, LANES), lambda l, s, tiles, order: (l, 0, tiles[s])),
+            scratch_shapes=[pltpu.VMEM((len(parts), second, rank, lanes), f32)],
+        ),
         out_shape=jax.ShapeDtypeStruct((blocks * lanes, rank, sources * second), f32),
+        input_output_aliases={2: 0} if earlier else {},
         compiler_params=pltpu.CompilerParams(vmem_limit_bytes=32 * MIB),
         name="turn",
-    )(parts)
+    )(tiles, order, *earlier, *parts)
 
 
 def shards(wide, narrow, tensor_slab, start_basis):
+    near = LANES // tensor_slab.shape[1]
+    me = lax.axis_index("wide")
+    order = (me ^ jnp.arange(wide)).astype(jnp.int32)
+    tiles = (me // near ^ jnp.arange(wide // near)).astype(jnp.int32)
+    places = order % near
     packed = total(local_gram(tensor_slab), wide, narrow)
-    basis = iterate(packed, start_basis.T)
-    parts = truncate(basis, tensor_slab, wide)
-    parts = lax.all_to_all(parts, "wide", split_axis=0, concat_axis=0, tiled=True)
-    return basis.T, turn(parts)
+    basis, *parts = iterate(order, packed, start_basis.T, tensor_slab)
+    first, rest = exchange(parts, wide, narrow, near)
+    field = turn(tiles[:1], places[:near], first, wide)
+    return basis.T, turn(tiles[1:], places[near:], rest, wide, field)
 
 
 def solution(mesh):

time: 148 us -> 126 us (0.85)
  the two profiles are of different devices: /device:TPU:8 before, /device:TPU:0 now
where the time goes in v2:
time: 126 us
  waiting for transfers between devices  52.4 us (42%)
  Pallas kernels  46.5 us (37%)
  starting transfers between devices  25.6 us (20%)
    ppermute x18, waiting for transfers between devices, swap(): lax.ppermute(x, ('wide', 'narrow'), [(i, i ^ mask) for i in range(devices)])  52.4 us
    pallas_call x1, Pallas kernels, iterate(): pl.pallas_call(iterate_kernel, in_specs=[pl.BlockSpec(memory_space=pltpu....  27.6 us
    ppermute x18, starting transfers between devices, swap(): lax.ppermute(x, ('wide', 'narrow'), [(i, i ^ mask) for i in range(devices)])  25.6 us
    pallas_call x1, Pallas kernels, local_gram(): pl.pallas_call(gram_kernel, grid=(second // depth, third // LANES), in_sp...  13.9 us
    pallas_call x2, Pallas kernels, turn(): pl.pallas_call(turn_kernel, grid_spec=pltpu.PrefetchScalarGridSpec(num_sc...  4.97 us
  transfers between devices with their start and end apart: 18, of which 14 were waited for; matrix products, arithmetic and copies ran while one was open for 1% of the time, Pallas kernels for 2%

profile of v2, /device:TPU:0, one launch (start us, length us, event | category | flops | bytes accessed | tf_op | source)
XLA Modules:
  0.0 126.2 jit_solution(10715979865553007176)
XLA Ops:
  0.6 13.9 %gram.1 = f32[1280,128]{1,0:T(8,128)S(1)} custom-call(f32[512,32,256]{2,1,0:T(8,128)} %slab_ref.1), custom_call_target="tpu_custom_call" | custom-call | tf_op jit(solution)/shard_map/gram/pallas_call | solution.py:96
  14.6 0.5 collective-permute-start
  15.1 1.3 collective-permute-done
  16.4 3.9 %collective-permute-start.3 = (f32[160,128]{1,0:T(8,128)S(1)}, f32[160,128]{1,0:T(8,128)S(1)}, u32[]{:S(2)}, u32[]{:S(2)}) collective-permute-start(f32[160,128]{1,0:T(8,128)S(1)} %get-tuple-element.34), channel_id=1, source_target_pairs={{0,6},{1,7},{2,4},{3,5},{4,2},{5,3},{6,0},{7,1},{8,14},{9,15},{10,... | collective-permute-start | bytes 245768 | tf_op jit(solution)/shard_map/ppermute | solution.py:111
  20.3 0.5 collective-permute-start.2
  20.8 0.1 collective-permute-start.1
  21.0 2.5 %collective-permute-done.3 = f32[160,128]{1,0:T(8,128)S(1)} collective-permute-done((f32[160,128]{1,0:T(8,128)S(1)}, f32[160,128]{1,0:T(8,128)S(1)}, u32[]{:S(2)}, u32[]{:S(2)}) %collective-permute-start.3) | collective-permute-done | bytes 81952 | tf_op jit(solution)/shard_map/ppermute | solution.py:111
  23.5 1.6 %collective-permute-done.2 = f32[160,128]{1,0:T(8,128)S(1)} collective-permute-done((f32[160,128]{1,0:T(8,128)S(1)}, f32[160,128]{1,0:T(8,128)S(1)}, u32[]{:S(2)}, u32[]{:S(2)}) %collective-permute-start.2) | collective-permute-done | bytes 81952 | tf_op jit(solution)/shard_map/ppermute | solution.py:111
  25.1 0.2 collective-permute-done.1
  25.3 0.0 copy-start
  25.3 3.7 %collective-permute-start.6 = (f32[160,128]{1,0:T(8,128)S(1)}, f32[160,128]{1,0:T(8,128)S(1)}, u32[]{:S(2)}, u32[]{:S(2)}) collective-permute-start(f32[160,128]{1,0:T(8,128)S(1)} %fusion), channel_id=1, source_target_pairs={{0,24},{1,25},{2,26},{3,27},{4,28},{5,29},{6,30},{7,31},{8,16},{9,... | collective-permute-start | bytes 245768 | tf_op jit(solution)/shard_map/ppermute | solution.py:111
  29.0 0.0 collective-permute-start.5
  29.0 0.8 collective-permute-start.4
  29.8 2.6 %collective-permute-done.6 = f32[160,128]{1,0:T(8,128)S(1)} collective-permute-done((f32[160,128]{1,0:T(8,128)S(1)}, f32[160,128]{1,0:T(8,128)S(1)}, u32[]{:S(2)}, u32[]{:S(2)}) %collective-permute-start.6) | collective-permute-done | bytes 81952 | tf_op jit(solution)/shard_map/ppermute | solution.py:111
  32.4 3.0 %collective-permute-done.5 = f32[160,128]{1,0:T(8,128)S(1)} collective-permute-done((f32[160,128]{1,0:T(8,128)S(1)}, f32[160,128]{1,0:T(8,128)S(1)}, u32[]{:S(2)}, u32[]{:S(2)}) %collective-permute-start.5) | collective-permute-done | bytes 81952 | tf_op jit(solution)/shard_map/ppermute | solution.py:111
  35.3 0.0 collective-permute-done.4
  35.4 2.5 %collective-permute-start.9 = (f32[160,128]{1,0:T(8,128)S(1)}, f32[160,128]{1,0:T(8,128)S(1)}, u32[]{:S(2)}, u32[]{:S(2)}) collective-permute-start(f32[160,128]{1,0:T(8,128)S(1)} %add_add_fusion), channel_id=1, source_target_pairs={{0,6},{1,7},{2,4},{3,5},{4,2},{5,3},{6,0},{7,1},{8,14},{9,15},{10,... | collective-permute-start | bytes 245768 | tf_op jit(solution)/shard_map/ppermute | solution.py:111
  37.9 0.8 collective-permute-start.8
  38.6 0.3 collective-permute-start.7
  38.9 2.8 %collective-permute-done.9 = f32[160,128]{1,0:T(8,128)S(1)} collective-permute-done((f32[160,128]{1,0:T(8,128)S(1)}, f32[160,128]{1,0:T(8,128)S(1)}, u32[]{:S(2)}, u32[]{:S(2)}) %collective-permute-start.9) | collective-permute-done | bytes 81952 | tf_op jit(solution)/shard_map/ppermute | solution.py:111
  41.7 0.9 collective-permute-done.8
  42.6 0.5 collective-permute-done.7
  43.1 0.1 collective-permute-start.10
  43.2 1.6 %collective-permute-done.10 = f32[640,128]{1,0:T(8,128)S(1)} collective-permute-done((f32[640,128]{1,0:T(8,128)S(1)}, f32[640,128]{1,0:T(8,128)S(1)}, u32[]{:S(2)}, u32[]{:S(2)}) %collective-permute-start.10) | collective-permute-done | bytes 327712 | tf_op jit(solution)/shard_map/ppermute | solution.py:111
  44.9 0.0 copy-done
  44.9 27.6 %iterate.1 = (f32[64,512]{1,0:T(8,128)}, f32[2,32,8,128]{3,2,1,0:T(8,128)S(1)}, f32[2,32,8,128]{3,2,1,0:T(8,128)S(1)}, f32[2,32,8,128]{3,2,1,0:T(8,128)S(1)}, f3...) custom-call(s32[8]{0:T(128)S(1)} %get-tuple-element.42.order_ref, ...), custom_call_target="tpu_custom_call" | custom-call | tf_op jit(solution)/shard_map/iterate/pallas_call | solution.py:264
  72.6 1.6 %collective-permute-start.11 = (f32[2,32,8,128]{3,2,1,0:T(8,128)S(1)}, f32[2,32,8,128]{3,2,1,0:T(8,128)S(1)}, u32[]{:S(2)}, u32[]{:S(2)}) collective-permute-start(f32[2,32,8,128]{3,2,1,0:T(8,128)S(1)} %get-tuple-element.17), channel_id=1, source_target_pairs={{0,12},{1,13},{2,14},{3,15},{4,8},{5,9},{6,10},{7,11},{8,4},{9,5},... | collective-permute-start | bytes 786440 | tf_op jit(solution)/shard_map/ppermute | solution.py:111
  74.2 0.6 collective-permute-start.12
  74.8 3.2 %collective-permute-start.15 = (f32[2,32,8,128]{3,2,1,0:T(8,128)S(1)}, f32[2,32,8,128]{3,2,1,0:T(8,128)S(1)}, u32[]{:S(2)}, u32[]{:S(2)}) collective-permute-start(f32[2,32,8,128]{3,2,1,0:T(8,128)S(1)} %get-tuple-element.25), channel_id=1, source_target_pairs={{0,20},{1,21},{2,22},{3,23},{4,16},{5,17},{6,18},{7,19},{8,28},{9,... | collective-permute-start | bytes 786440 | tf_op jit(solution)/shard_map/ppermute | solution.py:111
  78.0 1.1 collective-permute-start.16
  79.2 2.9 %collective-permute-start.17 = (f32[2,32,8,128]{3,2,1,0:T(8,128)S(1)}, f32[2,32,8,128]{3,2,1,0:T(8,128)S(1)}, u32[]{:S(2)}, u32[]{:S(2)}) collective-permute-start(f32[2,32,8,128]{3,2,1,0:T(8,128)S(1)} %get-tuple-element.27), channel_id=1, source_target_pairs={{0,28},{1,29},{2,30},{3,31},{4,24},{5,25},{6,26},{7,27},{8,20},{9,... | collective-permute-start | bytes 786440 | tf_op jit(solution)/shard_map/ppermute | solution.py:111
  82.0 3.8 %collective-permute-done.11.refs_3_ = f32[2,32,8,128]{3,2,1,0:T(8,128)S(1)} collective-permute-done((f32[2,32,8,128]{3,2,1,0:T(8,128)S(1)}, f32[2,32,8,128]{3,2,1,0:T(8,128)S(1)}, u32[]{:S(2)}, u32[]{:S(2)}) %collective-permute-start.11) | collective-permute-done | bytes 262176 | tf_op jit(solution)/shard_map/ppermute | solution.py:111
  85.9 5.5 %collective-permute-done.12.refs_1_ = f32[2,32,8,128]{3,2,1,0:T(8,128)S(1)} collective-permute-done((f32[2,32,8,128]{3,2,1,0:T(8,128)S(1)}, f32[2,32,8,128]{3,2,1,0:T(8,128)S(1)}, u32[]{:S(2)}, u32[]{:S(2)}) %collective-permute-start.12) | collective-permute-done | bytes 262176 | tf_op jit(solution)/shard_map/ppermute | solution.py:111
  91.4 2.5 %collective-permute-start.13 = (f32[2,32,8,128]{3,2,1,0:T(8,128)S(1)}, f32[2,32,8,128]{3,2,1,0:T(8,128)S(1)}, u32[]{:S(2)}, u32[]{:S(2)}) collective-permute-start(f32[2,32,8,128]{3,2,1,0:T(8,128)S(1)} %get-tuple-element.22), channel_id=1, source_target_pairs={{0,8},{1,9},{2,10},{3,11},{4,12},{5,13},{6,14},{7,15},{8,0},{9,1},... | collective-permute-start | bytes 786440 | tf_op jit(solution)/shard_map/ppermute | solution.py:111
  93.9 0.5 collective-permute-start.14
  94.4 0.6 fusion.3
  95.0 0.1 fusion.2
  95.1 11.8 %collective-permute-done.13.refs_2_ = f32[2,32,8,128]{3,2,1,0:T(8,128)S(1)} collective-permute-done((f32[2,32,8,128]{3,2,1,0:T(8,128)S(1)}, f32[2,32,8,128]{3,2,1,0:T(8,128)S(1)}, u32[]{:S(2)}, u32[]{:S(2)}) %collective-permute-start.13) | collective-permute-done | bytes 262176 | tf_op jit(solution)/shard_map/ppermute | solution.py:111
  106.9 2.5 %turn.2.refs_0_ = f32[256,8,256]{2,1,0:T(8,128)} custom-call(s32[1]{0:T(128)} %get-tuple-element.39.tiles_ref, s32[4]{0:T(128)S(1)} %get-tuple-element.37.order_ref, f32[2,32,8,128]{3,2,1,0:T(8,128)S(1)} %get-tuple-element.16.refs_0_, f32[2,32,8,128]{3,2,1,0:T(8,128)S(1)} %collective-permute-done.12.refs_1_, ...), custom_call_target="tpu_custom_call" | custom-call | tf_op jit(solution)/shard_map/turn/pallas_call | solution.py:322
  109.4 0.0 collective-permute-done.15.refs_2_
  109.4 0.0 collective-permute-done.16.refs_3_
  109.4 0.0 collective-permute-done.17.refs_4_
  109.4 14.3 %collective-permute-done.14.refs_1_ = f32[2,32,8,128]{3,2,1,0:T(8,128)S(1)} collective-permute-done((f32[2,32,8,128]{3,2,1,0:T(8,128)S(1)}, f32[2,32,8,128]{3,2,1,0:T(8,128)S(1)}, u32[]{:S(2)}, u32[]{:S(2)}) %collective-permute-start.14) | collective-permute-done | bytes 262176 | tf_op jit(solution)/shard_map/ppermute | solution.py:111
  123.8 2.4 %turn.3 = f32[256,8,256]{2,1,0:T(8,128)} custom-call(s32[1]{0:T(128)} %get-tuple-element.40.tiles_ref, s32[4]{0:T(128)S(1)} %get-tuple-element.38.order_ref, f32[256,8,256]{2,1,0:T(8,128)} %turn.2.refs_0_, f32[2,32,8,128]{3,2,1,0:T(8,128)S(1)} %collective-permute-done.14.refs_1_, ...), custom_call_target="tpu_custom_call", output_to_operand_aliasing={{}: (2, {})} | custom-call | tf_op jit(solution)/shard_map/turn/pallas_call | solution.py:322
  (11 shorter events, 0.3 us)
Async XLA Ops:
  14.6 1.8 %collective-permute-start = (f32[640,128]{1,0:T(8,128)S(1)}, f32[640,128]{1,0:T(8,128)S(1)}, u32[]{:S(2)}, u32[]{:S(2)}) collective-permute-start(f32[640,128]{1,0:T(8,128)S(1)} %dynamic-slice_bitcast_fusion), channel_id=1, source_target_pairs={{0,1},{1,0},{2,3},{3,2},{4,5},{5,4},{6,7},{7,6},{8,9},{9,8},{10,11... | collective-permute-start | bytes 983048 | tf_op jit(solution)/shard_map/ppermute | solution.py:111
  16.4 7.0 %collective-permute-start.3 = (f32[160,128]{1,0:T(8,128)S(1)}, f32[160,128]{1,0:T(8,128)S(1)}, u32[]{:S(2)}, u32[]{:S(2)}) collective-permute-start(f32[160,128]{1,0:T(8,128)S(1)} %get-tuple-element.34), channel_id=1, source_target_pairs={{0,6},{1,7},{2,4},{3,5},{4,2},{5,3},{6,0},{7,1},{8,14},{9,15},{10,... | collective-permute-start | bytes 245768 | tf_op jit(solution)/shard_map/ppermute | solution.py:111
  20.3 4.7 %collective-permute-start.2 = (f32[160,128]{1,0:T(8,128)S(1)}, f32[160,128]{1,0:T(8,128)S(1)}, u32[]{:S(2)}, u32[]{:S(2)}) collective-permute-start(f32[160,128]{1,0:T(8,128)S(1)} %get-tuple-element.35), channel_id=1, source_target_pairs={{0,4},{1,5},{2,6},{3,7},{4,0},{5,1},{6,2},{7,3},{8,12},{9,13},{10,... | collective-permute-start | bytes 245768 | tf_op jit(solution)/shard_map/ppermute | solution.py:111
  20.8 4.4 %collective-permute-start.1 = (f32[160,128]{1,0:T(8,128)S(1)}, f32[160,128]{1,0:T(8,128)S(1)}, u32[]{:S(2)}, u32[]{:S(2)}) collective-permute-start(f32[160,128]{1,0:T(8,128)S(1)} %get-tuple-element.36), channel_id=1, source_target_pairs={{0,2},{1,3},{2,0},{3,1},{4,6},{5,7},{6,4},{7,5},{8,10},{9,11},{10,... | collective-permute-start | bytes 245768 | tf_op jit(solution)/shard_map/ppermute | solution.py:111
  25.3 19.6 %copy-start = (f32[512,64]{0,1:T(8,128)S(1)}, f32[512,64]{0,1:T(8,128)}, u32[]{:S(2)}) copy-start(f32[512,64]{0,1:T(8,128)} %param.3) | copy-start | bytes 393220
  25.3 7.1 %collective-permute-start.6 = (f32[160,128]{1,0:T(8,128)S(1)}, f32[160,128]{1,0:T(8,128)S(1)}, u32[]{:S(2)}, u32[]{:S(2)}) collective-permute-start(f32[160,128]{1,0:T(8,128)S(1)} %fusion), channel_id=1, source_target_pairs={{0,24},{1,25},{2,26},{3,27},{4,28},{5,29},{6,30},{7,31},{8,16},{9,... | collective-permute-start | bytes 245768 | tf_op jit(solution)/shard_map/ppermute | solution.py:111
  29.0 6.3 %collective-permute-start.5 = (f32[160,128]{1,0:T(8,128)S(1)}, f32[160,128]{1,0:T(8,128)S(1)}, u32[]{:S(2)}, u32[]{:S(2)}) collective-permute-start(f32[160,128]{1,0:T(8,128)S(1)} %fusion), channel_id=1, source_target_pairs={{0,16},{1,17},{2,18},{3,19},{4,20},{5,21},{6,22},{7,23},{8,24},{9,... | collective-permute-start | bytes 245768 | tf_op jit(solution)/shard_map/ppermute | solution.py:111
  29.0 6.3 %collective-permute-start.4 = (f32[160,128]{1,0:T(8,128)S(1)}, f32[160,128]{1,0:T(8,128)S(1)}, u32[]{:S(2)}, u32[]{:S(2)}) collective-permute-start(f32[160,128]{1,0:T(8,128)S(1)} %fusion), channel_id=1, source_target_pairs={{0,8},{1,9},{2,10},{3,11},{4,12},{5,13},{6,14},{7,15},{8,0},{9,1},... | collective-permute-start | bytes 245768 | tf_op jit(solution)/shard_map/ppermute | solution.py:111
  35.4 6.3 %collective-permute-start.9 = (f32[160,128]{1,0:T(8,128)S(1)}, f32[160,128]{1,0:T(8,128)S(1)}, u32[]{:S(2)}, u32[]{:S(2)}) collective-permute-start(f32[160,128]{1,0:T(8,128)S(1)} %add_add_fusion), channel_id=1, source_target_pairs={{0,6},{1,7},{2,4},{3,5},{4,2},{5,3},{6,0},{7,1},{8,14},{9,15},{10,... | collective-permute-start | bytes 245768 | tf_op jit(solution)/shard_map/ppermute | solution.py:111
  37.9 4.7 %collective-permute-start.8 = (f32[160,128]{1,0:T(8,128)S(1)}, f32[160,128]{1,0:T(8,128)S(1)}, u32[]{:S(2)}, u32[]{:S(2)}) collective-permute-start(f32[160,128]{1,0:T(8,128)S(1)} %add_add_fusion), channel_id=1, source_target_pairs={{0,4},{1,5},{2,6},{3,7},{4,0},{5,1},{6,2},{7,3},{8,12},{9,13},{10,... | collective-permute-start | bytes 245768 | tf_op jit(solution)/shard_map/ppermute | solution.py:111
  38.6 4.4 %collective-permute-start.7 = (f32[160,128]{1,0:T(8,128)S(1)}, f32[160,128]{1,0:T(8,128)S(1)}, u32[]{:S(2)}, u32[]{:S(2)}) collective-permute-start(f32[160,128]{1,0:T(8,128)S(1)} %add_add_fusion), channel_id=1, source_target_pairs={{0,2},{1,3},{2,0},{3,1},{4,6},{5,7},{6,4},{7,5},{8,10},{9,11},{10,... | collective-permute-start | bytes 245768 | tf_op jit(solution)/shard_map/ppermute | solution.py:111
  43.1 1.7 %collective-permute-start.10 = (f32[640,128]{1,0:T(8,128)S(1)}, f32[640,128]{1,0:T(8,128)S(1)}, u32[]{:S(2)}, u32[]{:S(2)}) collective-permute-start(f32[640,128]{1,0:T(8,128)S(1)} %pad_maximum_fusion.1), channel_id=1, source_target_pairs={{0,1},{1,0},{2,3},{3,2},{4,5},{5,4},{6,7},{7,6},{8,9},{9,8},{10,11... | collective-permute-start | bytes 983048 | tf_op jit(solution)/shard_map/ppermute | solution.py:111
  72.6 13.3 %collective-permute-start.11 = (f32[2,32,8,128]{3,2,1,0:T(8,128)S(1)}, f32[2,32,8,128]{3,2,1,0:T(8,128)S(1)}, u32[]{:S(2)}, u32[]{:S(2)}) collective-permute-start(f32[2,32,8,128]{3,2,1,0:T(8,128)S(1)} %get-tuple-element.17), channel_id=1, source_target_pairs={{0,12},{1,13},{2,14},{3,15},{4,8},{5,9},{6,10},{7,11},{8,4},{9,5},... | collective-permute-start | bytes 786440 | tf_op jit(solution)/shard_map/ppermute | solution.py:111
  74.2 17.2 %collective-permute-start.12 = (f32[2,32,8,128]{3,2,1,0:T(8,128)S(1)}, f32[2,32,8,128]{3,2,1,0:T(8,128)S(1)}, u32[]{:S(2)}, u32[]{:S(2)}) collective-permute-start(f32[2,32,8,128]{3,2,1,0:T(8,128)S(1)} %get-tuple-element.18), channel_id=1, source_target_pairs={{0,4},{1,5},{2,6},{3,7},{4,0},{5,1},{6,2},{7,3},{8,12},{9,13},{10,... | collective-permute-start | bytes 786440 | tf_op jit(solution)/shard_map/ppermute | solution.py:111
  74.8 34.6 %collective-permute-start.15 = (f32[2,32,8,128]{3,2,1,0:T(8,128)S(1)}, f32[2,32,8,128]{3,2,1,0:T(8,128)S(1)}, u32[]{:S(2)}, u32[]{:S(2)}) collective-permute-start(f32[2,32,8,128]{3,2,1,0:T(8,128)S(1)} %get-tuple-element.25), channel_id=1, source_target_pairs={{0,20},{1,21},{2,22},{3,23},{4,16},{5,17},{6,18},{7,19},{8,28},{9,... | collective-permute-start | bytes 786440 | tf_op jit(solution)/shard_map/ppermute | solution.py:111
  78.0 31.4 %collective-permute-start.16 = (f32[2,32,8,128]{3,2,1,0:T(8,128)S(1)}, f32[2,32,8,128]{3,2,1,0:T(8,128)S(1)}, u32[]{:S(2)}, u32[]{:S(2)}) collective-permute-start(f32[2,32,8,128]{3,2,1,0:T(8,128)S(1)} %get-tuple-element.26), channel_id=1, source_target_pairs={{0,24},{1,25},{2,26},{3,27},{4,28},{5,29},{6,30},{7,31},{8,16},{9,... | collective-permute-start | bytes 786440 | tf_op jit(solution)/shard_map/ppermute | solution.py:111
  79.2 30.3 %collective-permute-start.17 = (f32[2,32,8,128]{3,2,1,0:T(8,128)S(1)}, f32[2,32,8,128]{3,2,1,0:T(8,128)S(1)}, u32[]{:S(2)}, u32[]{:S(2)}) collective-permute-start(f32[2,32,8,128]{3,2,1,0:T(8,128)S(1)} %get-tuple-element.27), channel_id=1, source_target_pairs={{0,28},{1,29},{2,30},{3,31},{4,24},{5,25},{6,26},{7,27},{8,20},{9,... | collective-permute-start | bytes 786440 | tf_op jit(solution)/shard_map/ppermute | solution.py:111
  91.4 15.5 %collective-permute-start.13 = (f32[2,32,8,128]{3,2,1,0:T(8,128)S(1)}, f32[2,32,8,128]{3,2,1,0:T(8,128)S(1)}, u32[]{:S(2)}, u32[]{:S(2)}) collective-permute-start(f32[2,32,8,128]{3,2,1,0:T(8,128)S(1)} %get-tuple-element.22), channel_id=1, source_target_pairs={{0,8},{1,9},{2,10},{3,11},{4,12},{5,13},{6,14},{7,15},{8,0},{9,1},... | collective-permute-start | bytes 786440 | tf_op jit(solution)/shard_map/ppermute | solution.py:111
  93.9 29.9 %collective-permute-start.14 = (f32[2,32,8,128]{3,2,1,0:T(8,128)S(1)}, f32[2,32,8,128]{3,2,1,0:T(8,128)S(1)}, u32[]{:S(2)}, u32[]{:S(2)}) collective-permute-start(f32[2,32,8,128]{3,2,1,0:T(8,128)S(1)} %get-tuple-element.24), channel_id=1, source_target_pairs={{0,16},{1,17},{2,18},{3,19},{4,20},{5,21},{6,22},{7,23},{8,24},{9,... | collective-permute-start | bytes 786440 | tf_op jit(solution)/shard_map/ppermute | solution.py:111

commit v3 on v2

--- a/solution.py
+++ b/solution.py
@@ -154,7 +154,7 @@
 
 
 def column_of(v, j):
-    return jnp.broadcast_to(v[:, j : j + 1], v.shape)
+    return jnp.take_along_axis(v, jnp.full(v.shape, j, jnp.int32), axis=1, mode="promise_in_bounds")
 
 
 def inverse_factor(inner, exact):
@@ -191,7 +191,7 @@
     return jnp.concatenate(out, axis=0)[:, n:]
 
 
-def iterate_kernel(order_ref, packed_ref, start_ref, slab_ref, basis_ref, *rest):
+def iterate_kernel(packed_ref, start_ref, slab_ref, basis_ref, *rest):
     *out_refs, high, low, by_group, slab, sems = rest
     blocks, strips, rows, depth, lanes = slab.shape
     copies = [
@@ -230,40 +230,41 @@
 
     rank = basis_ref.shape[0]
     size = rank // len(out_refs)
+    me = lax.axis_index("wide")
     for g in range(len(out_refs)):
         by_group[g] = basis_ref[g * size : (g + 1) * size]
-    basis = jnp.concatenate([by_group[order_ref[g]] for g in range(len(out_refs))], axis=0)
+    basis = jnp.concatenate([by_group[me ^ g] for g in range(len(out_refs))], axis=0)
     basis = jnp.concatenate(two(basis), axis=0)
     flat = slab.reshape(blocks * strips * rows * depth, lanes)
     for copy in copies:
         copy.wait()
 
     def columns(step, carry):
-        for j in range(0, depth, 2):
-            at = step * rows * depth + j
+        for j in range(0, 2 * depth, 2):
+            strip = step * 2 + j // depth
+            at = strip * rows * depth + j % depth
             pair = [two(flat[pl.ds(at + k, rows, stride=depth), :]) for k in range(2)]
             high_x, low_x = (jnp.concatenate(half, axis=1) for half in zip(*pair))
             by_high = dot(basis, high_x, NN)
             field = by_high[:rank] + (by_high[rank:] + dot(basis[:rank], low_x, NN))
             for k in range(2):
                 for g, out_ref in enumerate(out_refs):
-                    out_ref[step // strips, step % strips * depth + j + k] = field[
+                    out_ref[step * 2 // strips, step * 2 % strips * depth + j + k] = field[
                         g * size : (g + 1) * size, k * lanes : (k + 1) * lanes
                     ]
         return carry
 
-    lax.fori_loop(0, blocks * strips, columns, 0)
-
-
-def iterate(order, packed, start, tensor_slab):
+    lax.fori_loop(0, blocks * strips // 2, columns, 0)
+
+
+def iterate(packed, start, tensor_slab, groups):
     rank, n = start.shape
     rows, second, third = tensor_slab.shape
-    groups = order.shape[0]
     field = jax.ShapeDtypeStruct((third // LANES, second, rank // groups, LANES), f32)
     vmem = pl.BlockSpec(memory_space=pltpu.VMEM)
     return pl.pallas_call(
         iterate_kernel,
-        in_specs=[pl.BlockSpec(memory_space=pltpu.SMEM), vmem, vmem, pl.BlockSpec(memory_space=pl.ANY)],
+        in_specs=[vmem, vmem, pl.BlockSpec(memory_space=pl.ANY)],
         out_specs=[vmem] * (1 + groups),
         out_shape=[jax.ShapeDtypeStruct((rank, n), f32)] + [field] * groups,
         scratch_shapes=[pltpu.VMEM((n, n), bf16)] * 2
@@ -274,7 +275,7 @@
         ],
         compiler_params=pltpu.CompilerParams(vmem_limit_bytes=44 * MIB),
         name="iterate",
-    )(order, packed, start, tensor_slab)
+    )(packed, start, tensor_slab)
 
 
 def exchange(parts, wide, narrow, near):
@@ -282,70 +283,67 @@
         return swap(part, wide * narrow, mask * narrow)
 
     received = {0: parts[0]}
-    early = [*range(wide - 1, near, -1), *range(near - 1, 0, -2)]
-    for mask in early:
+    for mask in [*range(wide - 1, near - 1, -1), *range(1, near, 2)]:
         received[mask] = move(mask, parts[mask])
-    late = [mask for mask in range(near, 0, -1) if mask not in early]
-    *arrived, held = lax.optimization_barrier(
-        (*[received[mask] for mask in range(near - 1, 0, -2)], [parts[mask] for mask in late])
-    )
-    received.update(zip(range(near - 1, 0, -2), arrived))
+    late = range(2, near, 2)
+    received[1], held = lax.optimization_barrier((received[1], [parts[mask] for mask in late]))
     for mask, part in zip(late, held):
         received[mask] = move(mask, part)
-    return [received[mask] for mask in range(near)], [received[mask] for mask in range(near, wide)]
-
-
-def turn_kernel(tiles_ref, order_ref, *refs):
-    refs = refs[-2 - order_ref.shape[0] :]
-    *in_refs, out_ref, held = refs
-    _, second, rank, lanes = in_refs[0].shape
+    return [received[mask] for mask in range(wide)]
+
+
+def turn_kernel(*refs):
+    *in_refs, out_ref, held, turned, sems = refs
+    sources = len(in_refs)
+    _, second, rank, lanes = held.shape
     step = LANES // second
-    at = pl.program_id(1)
-
-    @pl.when(at == 0)
-    def _():
+    me = lax.axis_index("wide")
+    flat = held.reshape(sources * second * rank, lanes)
+    tiles = sources // step
+    copies = []
+    for block in range(in_refs[0].shape[0]):
         for s, in_ref in enumerate(in_refs):
-            held[s // step * step + order_ref[s]] = in_ref[0]
-
-    flat = held.reshape(len(in_refs) * second * rank, lanes)
-    flat_out = out_ref.reshape(lanes * rank, LANES)
-    first = at * (step * second * rank)
-    for r in range(rank):
-        rows = flat[pl.ds(first + r, step * second, stride=rank), :]
-        flat_out[pl.ds(r, lanes, stride=rank), :] = rows.T
-
-
-def turn(tiles, order, parts, sources, before=None):
+            held[s // step * step + (me ^ s) % step] = in_ref[block]
+        for tile in range(tiles):
+            index = block * tiles + tile
+            flat_out = turned.at[index].reshape(lanes * rank, LANES)
+            for r in range(rank):
+                rows = flat[pl.ds(tile * step * second * rank + r, step * second, stride=rank), :]
+                flat_out[pl.ds(r, lanes, stride=rank), :] = rows.T
+            columns = pl.ds(pl.multiple_of((me // step ^ tile) * LANES, LANES), LANES)
+            copy = pltpu.make_async_copy(
+                turned.at[index], out_ref.at[pl.ds(block * lanes, lanes), :, columns], sems.at[index]
+            )
+            copy.start()
+            copies.append(copy)
+    for copy in copies:
+        copy.wait()
+
+
+def turn(parts):
     blocks, second, rank, lanes = parts[0].shape
-    part = pl.BlockSpec((1, second, rank, lanes), lambda l, s, tiles, order: (l, 0, 0, 0))
-    earlier = [] if before is None else [before]
+    vmem, anywhere = (pl.BlockSpec(memory_space=space) for space in (pltpu.VMEM, pl.ANY))
+    pieces = blocks * len(parts) * second // LANES
     return pl.pallas_call(
         turn_kernel,
-        grid_spec=pltpu.PrefetchScalarGridSpec(
-            num_scalar_prefetch=2,
-            grid=(blocks, len(parts) * second // LANES),
-            in_specs=[pl.BlockSpec(memory_space=pl.ANY)] * len(earlier) + [part] * len(parts),
-            out_specs=pl.BlockSpec((lanes, rank, LANES), lambda l, s, tiles, order: (l, 0, tiles[s])),
-            scratch_shapes=[pltpu.VMEM((len(parts), second, rank, lanes), f32)],
-        ),
-        out_shape=jax.ShapeDtypeStruct((blocks * lanes, rank, sources * second), f32),
-        input_output_aliases={2: 0} if earlier else {},
+        in_specs=[vmem] * len(parts),
+        out_specs=anywhere,
+        out_shape=jax.ShapeDtypeStruct((blocks * lanes, rank, len(parts) * second), f32),
+        scratch_shapes=[
+            pltpu.VMEM((len(parts), second, rank, lanes), f32),
+            pltpu.VMEM((pieces, lanes, rank, LANES), f32),
+            pltpu.SemaphoreType.DMA((pieces,)),
+        ],
         compiler_params=pltpu.CompilerParams(vmem_limit_bytes=32 * MIB),
         name="turn",
-    )(tiles, order, *earlier, *parts)
+    )(*parts)
 
 
 def shards(wide, narrow, tensor_slab, start_basis):
     near = LANES // tensor_slab.shape[1]
-    me = lax.axis_index("wide")
-    order = (me ^ jnp.arange(wide)).astype(jnp.int32)
-    tiles = (me // near ^ jnp.arange(wide // near)).astype(jnp.int32)
-    places = order % near
     packed = total(local_gram(tensor_slab), wide, narrow)
-    basis, *parts = iterate(order, packed, start_basis.T, tensor_slab)
-    first, rest = exchange(parts, wide, narrow, near)
-    field = turn(tiles[:1], places[:near], first, wide)
-    return basis.T, turn(tiles[1:], places[near:], rest, wide, field)
+    basis, *parts = iterate(packed, start_basis.T, tensor_slab, wide)
+    return basis.T, turn(exchange(parts, wide, narrow, near))
 
 
 def solution(mesh):

time: 126 us -> 120 us (0.952)
  the two profiles are of different devices: /device:TPU:0 before, /device:TPU:8 now
where the time goes in v3:
time: 120 us
  waiting for transfers between devices  57.2 us (48%)
  Pallas kernels  40.2 us (34%)
  starting transfers between devices  21.5 us (18%)
    ppermute x18, waiting for transfers between devices, swap(): lax.ppermute(x, ('wide', 'narrow'), [(i, i ^ mask) for i in range(devices)])  57.2 us
    pallas_call x1, Pallas kernels, iterate(): pl.pallas_call(iterate_kernel, in_specs=[vmem, vmem, pl.BlockSpec(memory_...  24.7 us
    ppermute x18, starting transfers between devices, swap(): lax.ppermute(x, ('wide', 'narrow'), [(i, i ^ mask) for i in range(devices)])  21.5 us
    pallas_call x1, Pallas kernels, local_gram(): pl.pallas_call(gram_kernel, grid=(second // depth, third // LANES), in_sp...  13.9 us
  transfers between devices with their start and end apart: 18, of which 16 were waited for; matrix products, arithmetic and copies ran while one was open for 0% of the time, Pallas kernels for 0%

profile of v3, /device:TPU:8, one launch (start us, length us, event | category | flops | bytes accessed | tf_op | source)
XLA Modules:
  0.0 120.1 jit_solution(3082952389611020577)
XLA Ops:
  0.6 0.0 copy-start
  0.7 13.9 %gram.1 = f32[1280,128]{1,0:T(8,128)S(1)} custom-call(f32[512,32,256]{2,1,0:T(8,128)} %slab_ref.1), custom_call_target="tpu_custom_call" | custom-call | tf_op jit(solution)/shard_map/gram/pallas_call | solution.py:96
  14.6 0.1 collective-permute-start
  14.7 1.6 %collective-permute-done = f32[640,128]{1,0:T(8,128)S(1)} collective-permute-done((f32[640,128]{1,0:T(8,128)S(1)}, f32[640,128]{1,0:T(8,128)S(1)}, u32[]{:S(2)}, u32[]{:S(2)}) %collective-permute-start) | collective-permute-done | bytes 327712 | tf_op jit(solution)/shard_map/ppermute | solution.py:111
  16.4 2.5 %collective-permute-start.3 = (f32[160,128]{1,0:T(8,128)S(1)}, f32[160,128]{1,0:T(8,128)S(1)}, u32[]{:S(2)}, u32[]{:S(2)}) collective-permute-start(f32[160,128]{1,0:T(8,128)S(1)} %get-tuple-element.30), channel_id=1, source_target_pairs={{0,6},{1,7},{2,4},{3,5},{4,2},{5,3},{6,0},{7,1},{8,14},{9,15},{10,... | collective-permute-start | bytes 245768 | tf_op jit(solution)/shard_map/ppermute | solution.py:111
  18.9 0.5 collective-permute-start.2
  19.4 0.5 collective-permute-start.1
  19.9 2.4 %collective-permute-done.3 = f32[160,128]{1,0:T(8,128)S(1)} collective-permute-done((f32[160,128]{1,0:T(8,128)S(1)}, f32[160,128]{1,0:T(8,128)S(1)}, u32[]{:S(2)}, u32[]{:S(2)}) %collective-permute-start.3) | collective-permute-done | bytes 81952 | tf_op jit(solution)/shard_map/ppermute | solution.py:111
  22.4 1.3 %collective-permute-done.2 = f32[160,128]{1,0:T(8,128)S(1)} collective-permute-done((f32[160,128]{1,0:T(8,128)S(1)}, f32[160,128]{1,0:T(8,128)S(1)}, u32[]{:S(2)}, u32[]{:S(2)}) %collective-permute-start.2) | collective-permute-done | bytes 81952 | tf_op jit(solution)/shard_map/ppermute | solution.py:111
  23.7 0.2 collective-permute-done.1
  23.9 1.6 %collective-permute-start.6 = (f32[160,128]{1,0:T(8,128)S(1)}, f32[160,128]{1,0:T(8,128)S(1)}, u32[]{:S(2)}, u32[]{:S(2)}) collective-permute-start(f32[160,128]{1,0:T(8,128)S(1)} %fusion), channel_id=1, source_target_pairs={{0,24},{1,25},{2,26},{3,27},{4,28},{5,29},{6,30},{7,31},{8,16},{9,... | collective-permute-start | bytes 245768 | tf_op jit(solution)/shard_map/ppermute | solution.py:111
  25.5 1.2 %collective-permute-start.5 = (f32[160,128]{1,0:T(8,128)S(1)}, f32[160,128]{1,0:T(8,128)S(1)}, u32[]{:S(2)}, u32[]{:S(2)}) collective-permute-start(f32[160,128]{1,0:T(8,128)S(1)} %fusion), channel_id=1, source_target_pairs={{0,16},{1,17},{2,18},{3,19},{4,20},{5,21},{6,22},{7,23},{8,24},{9,... | collective-permute-start | bytes 245768 | tf_op jit(solution)/shard_map/ppermute | solution.py:111
  26.8 1.2 %collective-permute-start.4 = (f32[160,128]{1,0:T(8,128)S(1)}, f32[160,128]{1,0:T(8,128)S(1)}, u32[]{:S(2)}, u32[]{:S(2)}) collective-permute-start(f32[160,128]{1,0:T(8,128)S(1)} %fusion), channel_id=1, source_target_pairs={{0,8},{1,9},{2,10},{3,11},{4,12},{5,13},{6,14},{7,15},{8,0},{9,1},... | collective-permute-start | bytes 245768 | tf_op jit(solution)/shard_map/ppermute | solution.py:111
  28.0 3.4 %collective-permute-done.6 = f32[160,128]{1,0:T(8,128)S(1)} collective-permute-done((f32[160,128]{1,0:T(8,128)S(1)}, f32[160,128]{1,0:T(8,128)S(1)}, u32[]{:S(2)}, u32[]{:S(2)}) %collective-permute-start.6) | collective-permute-done | bytes 81952 | tf_op jit(solution)/shard_map/ppermute | solution.py:111
  31.4 0.8 collective-permute-done.5
  32.2 1.0 collective-permute-done.4
  33.2 2.5 %collective-permute-start.9 = (f32[160,128]{1,0:T(8,128)S(1)}, f32[160,128]{1,0:T(8,128)S(1)}, u32[]{:S(2)}, u32[]{:S(2)}) collective-permute-start(f32[160,128]{1,0:T(8,128)S(1)} %add_add_fusion), channel_id=1, source_target_pairs={{0,6},{1,7},{2,4},{3,5},{4,2},{5,3},{6,0},{7,1},{8,14},{9,15},{10,... | collective-permute-start | bytes 245768 | tf_op jit(solution)/shard_map/ppermute | solution.py:111
  35.7 0.7 collective-permute-start.8
  36.4 0.4 collective-permute-start.7
  36.8 2.0 %collective-permute-done.9 = f32[160,128]{1,0:T(8,128)S(1)} collective-permute-done((f32[160,128]{1,0:T(8,128)S(1)}, f32[160,128]{1,0:T(8,128)S(1)}, u32[]{:S(2)}, u32[]{:S(2)}) %collective-permute-start.9) | collective-permute-done | bytes 81952 | tf_op jit(solution)/shard_map/ppermute | solution.py:111
  38.7 1.4 %collective-permute-done.8 = f32[160,128]{1,0:T(8,128)S(1)} collective-permute-done((f32[160,128]{1,0:T(8,128)S(1)}, f32[160,128]{1,0:T(8,128)S(1)}, u32[]{:S(2)}, u32[]{:S(2)}) %collective-permute-start.8) | collective-permute-done | bytes 81952 | tf_op jit(solution)/shard_map/ppermute | solution.py:111
  40.2 0.7 collective-permute-done.7
  40.9 0.1 collective-permute-start.10
  41.0 1.6 %collective-permute-done.10 = f32[640,128]{1,0:T(8,128)S(1)} collective-permute-done((f32[640,128]{1,0:T(8,128)S(1)}, f32[640,128]{1,0:T(8,128)S(1)}, u32[]{:S(2)}, u32[]{:S(2)}) %collective-permute-start.10) | collective-permute-done | bytes 327712 | tf_op jit(solution)/shard_map/ppermute | solution.py:111
  42.7 0.0 copy-done
  42.7 24.7 %iterate.1 = (f32[64,512]{1,0:T(8,128)}, f32[2,32,8,128]{3,2,1,0:T(8,128)S(1)}, f32[2,32,8,128]{3,2,1,0:T(8,128)S(1)}, f32[2,32,8,128]{3,2,1,0:T(8,128)S(1)}, f3...) custom-call(f32[1280,128]{1,0:T(8,128)S(1)} %pad_maximum_fusion.pack, ...), custom_call_target="tpu_custom_call" | custom-call | tf_op jit(solution)/shard_map/iterate/pallas_call | solution.py:265
  67.4 1.4 %collective-permute-start.11 = (f32[2,32,8,128]{3,2,1,0:T(8,128)S(1)}, f32[2,32,8,128]{3,2,1,0:T(8,128)S(1)}, u32[]{:S(2)}, u32[]{:S(2)}) collective-permute-start(f32[2,32,8,128]{3,2,1,0:T(8,128)S(1)} %get-tuple-element.15), channel_id=1, source_target_pairs={{0,4},{1,5},{2,6},{3,7},{4,0},{5,1},{6,2},{7,3},{8,12},{9,13},{10,... | collective-permute-start | bytes 786440 | tf_op jit(solution)/shard_map/ppermute | solution.py:111
  68.8 1.3 %collective-permute-start.13 = (f32[2,32,8,128]{3,2,1,0:T(8,128)S(1)}, f32[2,32,8,128]{3,2,1,0:T(8,128)S(1)}, u32[]{:S(2)}, u32[]{:S(2)}) collective-permute-start(f32[2,32,8,128]{3,2,1,0:T(8,128)S(1)} %get-tuple-element.19), channel_id=1, source_target_pairs={{0,12},{1,13},{2,14},{3,15},{4,8},{5,9},{6,10},{7,11},{8,4},{9,5},... | collective-permute-start | bytes 786440 | tf_op jit(solution)/shard_map/ppermute | solution.py:111
  70.1 1.0 collective-permute-start.14
  71.1 2.7 %collective-permute-start.15 = (f32[2,32,8,128]{3,2,1,0:T(8,128)S(1)}, f32[2,32,8,128]{3,2,1,0:T(8,128)S(1)}, u32[]{:S(2)}, u32[]{:S(2)}) collective-permute-start(f32[2,32,8,128]{3,2,1,0:T(8,128)S(1)} %get-tuple-element.21), channel_id=1, source_target_pairs={{0,20},{1,21},{2,22},{3,23},{4,16},{5,17},{6,18},{7,19},{8,28},{9,... | collective-permute-start | bytes 786440 | tf_op jit(solution)/shard_map/ppermute | solution.py:111
  73.8 1.7 %collective-permute-start.16 = (f32[2,32,8,128]{3,2,1,0:T(8,128)S(1)}, f32[2,32,8,128]{3,2,1,0:T(8,128)S(1)}, u32[]{:S(2)}, u32[]{:S(2)}) collective-permute-start(f32[2,32,8,128]{3,2,1,0:T(8,128)S(1)} %get-tuple-element.22), channel_id=1, source_target_pairs={{0,24},{1,25},{2,26},{3,27},{4,28},{5,29},{6,30},{7,31},{8,16},{9,... | collective-permute-start | bytes 786440 | tf_op jit(solution)/shard_map/ppermute | solution.py:111
  75.5 5.9 %collective-permute-done.11.refs_1_ = f32[2,32,8,128]{3,2,1,0:T(8,128)S(1)} collective-permute-done((f32[2,32,8,128]{3,2,1,0:T(8,128)S(1)}, f32[2,32,8,128]{3,2,1,0:T(8,128)S(1)}, u32[]{:S(2)}, u32[]{:S(2)}) %collective-permute-start.11) | collective-permute-done | bytes 262176 | tf_op jit(solution)/shard_map/ppermute | solution.py:111
  81.4 1.3 %collective-permute-start.17 = (f32[2,32,8,128]{3,2,1,0:T(8,128)S(1)}, f32[2,32,8,128]{3,2,1,0:T(8,128)S(1)}, u32[]{:S(2)}, u32[]{:S(2)}) collective-permute-start(f32[2,32,8,128]{3,2,1,0:T(8,128)S(1)} %get-tuple-element.23), channel_id=1, source_target_pairs={{0,28},{1,29},{2,30},{3,31},{4,24},{5,25},{6,26},{7,27},{8,20},{9,... | collective-permute-start | bytes 786440 | tf_op jit(solution)/shard_map/ppermute | solution.py:111
  82.7 0.0 collective-permute-done.13.refs_3_
  82.7 0.7 collective-permute-start.12
  83.5 16.7 %collective-permute-done.14.refs_4_ = f32[2,32,8,128]{3,2,1,0:T(8,128)S(1)} collective-permute-done((f32[2,32,8,128]{3,2,1,0:T(8,128)S(1)}, f32[2,32,8,128]{3,2,1,0:T(8,128)S(1)}, u32[]{:S(2)}, u32[]{:S(2)}) %collective-permute-start.14) | collective-permute-done | bytes 262176 | tf_op jit(solution)/shard_map/ppermute | solution.py:111
  100.2 5.8 %collective-permute-done.15.refs_5_ = f32[2,32,8,128]{3,2,1,0:T(8,128)S(1)} collective-permute-done((f32[2,32,8,128]{3,2,1,0:T(8,128)S(1)}, f32[2,32,8,128]{3,2,1,0:T(8,128)S(1)}, u32[]{:S(2)}, u32[]{:S(2)}) %collective-permute-start.15) | collective-permute-done | bytes 262176 | tf_op jit(solution)/shard_map/ppermute | solution.py:111
  106.0 7.4 %collective-permute-done.16.refs_6_ = f32[2,32,8,128]{3,2,1,0:T(8,128)S(1)} collective-permute-done((f32[2,32,8,128]{3,2,1,0:T(8,128)S(1)}, f32[2,32,8,128]{3,2,1,0:T(8,128)S(1)}, u32[]{:S(2)}, u32[]{:S(2)}) %collective-permute-start.16) | collective-permute-done | bytes 262176 | tf_op jit(solution)/shard_map/ppermute | solution.py:111
  113.4 5.0 %collective-permute-done.17.refs_7_ = f32[2,32,8,128]{3,2,1,0:T(8,128)S(1)} collective-permute-done((f32[2,32,8,128]{3,2,1,0:T(8,128)S(1)}, f32[2,32,8,128]{3,2,1,0:T(8,128)S(1)}, u32[]{:S(2)}, u32[]{:S(2)}) %collective-permute-start.17) | collective-permute-done | bytes 262176 | tf_op jit(solution)/shard_map/ppermute | solution.py:111
  118.4 0.0 collective-permute-done.12.refs_2_
  118.4 1.7 %turn.1 = f32[256,8,256]{2,1,0:T(8,128)} custom-call(f32[2,32,8,128]{3,2,1,0:T(8,128)S(1)} %get-tuple-element.14.refs_0_, f32[2,32,8,128]{3,2,1,0:T(8,128)S(1)} %collective-permute-done.11.refs_1_, f32[2,32,8,128]{3,2,1,0:T(8,128)S(1)} %collective-permute-done.12.refs_2_, f32[2,32,8,128]{3,2,1,0:T(8,128)S(1)} %collective-permute-done.13.refs_3_, ...), custom_call_target="tpu_custom_call" | custom-call | tf_op jit(solution)/shard_map/turn/pallas_call | solution.py:327
  (9 shorter events, 0.3 us)
Async XLA Ops:
  0.6 42.1 %copy-start = (f32[512,64]{0,1:T(8,128)S(1)}, f32[512,64]{0,1:T(8,128)}, u32[]{:S(2)}) copy-start(f32[512,64]{0,1:T(8,128)} %param.3) | copy-start | bytes 393220
  14.6 1.7 %collective-permute-start = (f32[640,128]{1,0:T(8,128)S(1)}, f32[640,128]{1,0:T(8,128)S(1)}, u32[]{:S(2)}, u32[]{:S(2)}) collective-permute-start(f32[640,128]{1,0:T(8,128)S(1)} %dynamic-slice_bitcast_fusion), channel_id=1, source_target_pairs={{0,1},{1,0},{2,3},{3,2},{4,5},{5,4},{6,7},{7,6},{8,9},{9,8},{10,11... | collective-permute-start | bytes 983048 | tf_op jit(solution)/shard_map/ppermute | solution.py:111
  16.4 6.0 %collective-permute-start.3 = (f32[160,128]{1,0:T(8,128)S(1)}, f32[160,128]{1,0:T(8,128)S(1)}, u32[]{:S(2)}, u32[]{:S(2)}) collective-permute-start(f32[160,128]{1,0:T(8,128)S(1)} %get-tuple-element.30), channel_id=1, source_target_pairs={{0,6},{1,7},{2,4},{3,5},{4,2},{5,3},{6,0},{7,1},{8,14},{9,15},{10,... | collective-permute-start | bytes 245768 | tf_op jit(solution)/shard_map/ppermute | solution.py:111
  18.9 4.8 %collective-permute-start.2 = (f32[160,128]{1,0:T(8,128)S(1)}, f32[160,128]{1,0:T(8,128)S(1)}, u32[]{:S(2)}, u32[]{:S(2)}) collective-permute-start(f32[160,128]{1,0:T(8,128)S(1)} %get-tuple-element.31), channel_id=1, source_target_pairs={{0,4},{1,5},{2,6},{3,7},{4,0},{5,1},{6,2},{7,3},{8,12},{9,13},{10,... | collective-permute-start | bytes 245768 | tf_op jit(solution)/shard_map/ppermute | solution.py:111
  19.4 4.4 %collective-permute-start.1 = (f32[160,128]{1,0:T(8,128)S(1)}, f32[160,128]{1,0:T(8,128)S(1)}, u32[]{:S(2)}, u32[]{:S(2)}) collective-permute-start(f32[160,128]{1,0:T(8,128)S(1)} %get-tuple-element.32), channel_id=1, source_target_pairs={{0,2},{1,3},{2,0},{3,1},{4,6},{5,7},{6,4},{7,5},{8,10},{9,11},{10,... | collective-permute-start | bytes 245768 | tf_op jit(solution)/shard_map/ppermute | solution.py:111
  23.9 7.5 %collective-permute-start.6 = (f32[160,128]{1,0:T(8,128)S(1)}, f32[160,128]{1,0:T(8,128)S(1)}, u32[]{:S(2)}, u32[]{:S(2)}) collective-permute-start(f32[160,128]{1,0:T(8,128)S(1)} %fusion), channel_id=1, source_target_pairs={{0,24},{1,25},{2,26},{3,27},{4,28},{5,29},{6,30},{7,31},{8,16},{9,... | collective-permute-start | bytes 245768 | tf_op jit(solution)/shard_map/ppermute | solution.py:111
  25.5 6.7 %collective-permute-start.5 = (f32[160,128]{1,0:T(8,128)S(1)}, f32[160,128]{1,0:T(8,128)S(1)}, u32[]{:S(2)}, u32[]{:S(2)}) collective-permute-start(f32[160,128]{1,0:T(8,128)S(1)} %fusion), channel_id=1, source_target_pairs={{0,16},{1,17},{2,18},{3,19},{4,20},{5,21},{6,22},{7,23},{8,24},{9,... | collective-permute-start | bytes 245768 | tf_op jit(solution)/shard_map/ppermute | solution.py:111
  26.8 6.4 %collective-permute-start.4 = (f32[160,128]{1,0:T(8,128)S(1)}, f32[160,128]{1,0:T(8,128)S(1)}, u32[]{:S(2)}, u32[]{:S(2)}) collective-permute-start(f32[160,128]{1,0:T(8,128)S(1)} %fusion), channel_id=1, source_target_pairs={{0,8},{1,9},{2,10},{3,11},{4,12},{5,13},{6,14},{7,15},{8,0},{9,1},... | collective-permute-start | bytes 245768 | tf_op jit(solution)/shard_map/ppermute | solution.py:111
  33.2 5.5 %collective-permute-start.9 = (f32[160,128]{1,0:T(8,128)S(1)}, f32[160,128]{1,0:T(8,128)S(1)}, u32[]{:S(2)}, u32[]{:S(2)}) collective-permute-start(f32[160,128]{1,0:T(8,128)S(1)} %add_add_fusion), channel_id=1, source_target_pairs={{0,6},{1,7},{2,4},{3,5},{4,2},{5,3},{6,0},{7,1},{8,14},{9,15},{10,... | collective-permute-start | bytes 245768 | tf_op jit(solution)/shard_map/ppermute | solution.py:111
  35.7 4.4 %collective-permute-start.8 = (f32[160,128]{1,0:T(8,128)S(1)}, f32[160,128]{1,0:T(8,128)S(1)}, u32[]{:S(2)}, u32[]{:S(2)}) collective-permute-start(f32[160,128]{1,0:T(8,128)S(1)} %add_add_fusion), channel_id=1, source_target_pairs={{0,4},{1,5},{2,6},{3,7},{4,0},{5,1},{6,2},{7,3},{8,12},{9,13},{10,... | collective-permute-start | bytes 245768 | tf_op jit(solution)/shard_map/ppermute | solution.py:111
  36.4 4.4 %collective-permute-start.7 = (f32[160,128]{1,0:T(8,128)S(1)}, f32[160,128]{1,0:T(8,128)S(1)}, u32[]{:S(2)}, u32[]{:S(2)}) collective-permute-start(f32[160,128]{1,0:T(8,128)S(1)} %add_add_fusion), channel_id=1, source_target_pairs={{0,2},{1,3},{2,0},{3,1},{4,6},{5,7},{6,4},{7,5},{8,10},{9,11},{10,... | collective-permute-start | bytes 245768 | tf_op jit(solution)/shard_map/ppermute | solution.py:111
  40.9 1.7 %collective-permute-start.10 = (f32[640,128]{1,0:T(8,128)S(1)}, f32[640,128]{1,0:T(8,128)S(1)}, u32[]{:S(2)}, u32[]{:S(2)}) collective-permute-start(f32[640,128]{1,0:T(8,128)S(1)} %pad_maximum_fusion.1), channel_id=1, source_target_pairs={{0,1},{1,0},{2,3},{3,2},{4,5},{5,4},{6,7},{7,6},{8,9},{9,8},{10,11... | collective-permute-start | bytes 983048 | tf_op jit(solution)/shard_map/ppermute | solution.py:111
  67.4 14.0 %collective-permute-start.11 = (f32[2,32,8,128]{3,2,1,0:T(8,128)S(1)}, f32[2,32,8,128]{3,2,1,0:T(8,128)S(1)}, u32[]{:S(2)}, u32[]{:S(2)}) collective-permute-start(f32[2,32,8,128]{3,2,1,0:T(8,128)S(1)} %get-tuple-element.15), channel_id=1, source_target_pairs={{0,4},{1,5},{2,6},{3,7},{4,0},{5,1},{6,2},{7,3},{8,12},{9,13},{10,... | collective-permute-start | bytes 786440 | tf_op jit(solution)/shard_map/ppermute | solution.py:111
  68.8 13.9 %collective-permute-start.13 = (f32[2,32,8,128]{3,2,1,0:T(8,128)S(1)}, f32[2,32,8,128]{3,2,1,0:T(8,128)S(1)}, u32[]{:S(2)}, u32[]{:S(2)}) collective-permute-start(f32[2,32,8,128]{3,2,1,0:T(8,128)S(1)} %get-tuple-element.19), channel_id=1, source_target_pairs={{0,12},{1,13},{2,14},{3,15},{4,8},{5,9},{6,10},{7,11},{8,4},{9,5},... | collective-permute-start | bytes 786440 | tf_op jit(solution)/shard_map/ppermute | solution.py:111
  70.1 30.1 %collective-permute-start.14 = (f32[2,32,8,128]{3,2,1,0:T(8,128)S(1)}, f32[2,32,8,128]{3,2,1,0:T(8,128)S(1)}, u32[]{:S(2)}, u32[]{:S(2)}) collective-permute-start(f32[2,32,8,128]{3,2,1,0:T(8,128)S(1)} %get-tuple-element.20), channel_id=1, source_target_pairs={{0,16},{1,17},{2,18},{3,19},{4,20},{5,21},{6,22},{7,23},{8,24},{9,... | collective-permute-start | bytes 786440 | tf_op jit(solution)/shard_map/ppermute | solution.py:111
  71.1 34.8 %collective-permute-start.15 = (f32[2,32,8,128]{3,2,1,0:T(8,128)S(1)}, f32[2,32,8,128]{3,2,1,0:T(8,128)S(1)}, u32[]{:S(2)}, u32[]{:S(2)}) collective-permute-start(f32[2,32,8,128]{3,2,1,0:T(8,128)S(1)} %get-tuple-element.21), channel_id=1, source_target_pairs={{0,20},{1,21},{2,22},{3,23},{4,16},{5,17},{6,18},{7,19},{8,28},{9,... | collective-permute-start | bytes 786440 | tf_op jit(solution)/shard_map/ppermute | solution.py:111
  73.8 39.6 %collective-permute-start.16 = (f32[2,32,8,128]{3,2,1,0:T(8,128)S(1)}, f32[2,32,8,128]{3,2,1,0:T(8,128)S(1)}, u32[]{:S(2)}, u32[]{:S(2)}) collective-permute-start(f32[2,32,8,128]{3,2,1,0:T(8,128)S(1)} %get-tuple-element.22), channel_id=1, source_target_pairs={{0,24},{1,25},{2,26},{3,27},{4,28},{5,29},{6,30},{7,31},{8,16},{9,... | collective-permute-start | bytes 786440 | tf_op jit(solution)/shard_map/ppermute | solution.py:111
  81.4 37.0 %collective-permute-start.17 = (f32[2,32,8,128]{3,2,1,0:T(8,128)S(1)}, f32[2,32,8,128]{3,2,1,0:T(8,128)S(1)}, u32[]{:S(2)}, u32[]{:S(2)}) collective-permute-start(f32[2,32,8,128]{3,2,1,0:T(8,128)S(1)} %get-tuple-element.23), channel_id=1, source_target_pairs={{0,28},{1,29},{2,30},{3,31},{4,24},{5,25},{6,26},{7,27},{8,20},{9,... | collective-permute-start | bytes 786440 | tf_op jit(solution)/shard_map/ppermute | solution.py:111
  82.7 35.6 %collective-permute-start.12 = (f32[2,32,8,128]{3,2,1,0:T(8,128)S(1)}, f32[2,32,8,128]{3,2,1,0:T(8,128)S(1)}, u32[]{:S(2)}, u32[]{:S(2)}) collective-permute-start(f32[2,32,8,128]{3,2,1,0:T(8,128)S(1)} %get-tuple-element.18), channel_id=1, source_target_pairs={{0,8},{1,9},{2,10},{3,11},{4,12},{5,13},{6,14},{7,15},{8,0},{9,1},... | collective-permute-start | bytes 786440 | tf_op jit(solution)/shard_map/ppermute | solution.py:111

commit v4 on v3

--- a/solution.py
+++ b/solution.py
@@ -218,9 +218,10 @@
 
     def sweep(_, carry):
         block = two(basis_ref[...])
-        product = times_gram(block)
-        inverse = inverse_factor(dot_two(block, block, NT), False)
-        basis_ref[...] = dot_two(two(inverse), two(product), NN)
+        inner = dot_two(block, block, NT)
+        product = two(times_gram(block))
+        inverse = inverse_factor(inner, False)
+        basis_ref[...] = dot_two(two(inverse), product, NN)
         return carry
 
     lax.fori_loop(0, ITERS - 1, sweep, 0)

time: 120 us -> 119 us (level)
  Pallas kernels: 40.2 us -> 38.9 us
    pallas_call x1, Pallas kernels: 24.7 us -> 23.3 us  [iterate(): pl.pallas_call(iterate_kernel, in_specs=[vmem, vmem, pl.BlockSpec(memory_...]
where the time goes in v4:
time: 119 us
  waiting for transfers between devices  57 us (48%)
  Pallas kernels  38.9 us (33%)
  starting transfers between devices  21.7 us (18%)
    ppermute x18, waiting for transfers between devices, swap(): lax.ppermute(x, ('wide', 'narrow'), [(i, i ^ mask) for i in range(devices)])  57 us
    pallas_call x1, Pallas kernels, iterate(): pl.pallas_call(iterate_kernel, in_specs=[vmem, vmem, pl.BlockSpec(memory_...  23.3 us
    ppermute x18, starting transfers between devices, swap(): lax.ppermute(x, ('wide', 'narrow'), [(i, i ^ mask) for i in range(devices)])  21.7 us
    pallas_call x1, Pallas kernels, local_gram(): pl.pallas_call(gram_kernel, grid=(second // depth, third // LANES), in_sp...  13.9 us
  transfers between devices with their start and end apart: 18, of which 16 were waited for; matrix products, arithmetic and copies ran while one was open for 0% of the time, Pallas kernels for 0%

profile of v4, /device:TPU:8, one launch (start us, length us, event | category | flops | bytes accessed | tf_op | source)
XLA Modules:
  0.0 118.7 jit_solution(16364196754922706985)
XLA Ops:
  0.6 0.0 copy-start
  0.7 13.9 %gram.1 = f32[1280,128]{1,0:T(8,128)S(1)} custom-call(f32[512,32,256]{2,1,0:T(8,128)} %slab_ref.1), custom_call_target="tpu_custom_call" | custom-call | tf_op jit(solution)/shard_map/gram/pallas_call | solution.py:96
  14.6 0.1 collective-permute-start
  14.7 1.6 %collective-permute-done = f32[640,128]{1,0:T(8,128)S(1)} collective-permute-done((f32[640,128]{1,0:T(8,128)S(1)}, f32[640,128]{1,0:T(8,128)S(1)}, u32[]{:S(2)}, u32[]{:S(2)}) %collective-permute-start) | collective-permute-done | bytes 327712 | tf_op jit(solution)/shard_map/ppermute | solution.py:111
  16.4 2.5 %collective-permute-start.3 = (f32[160,128]{1,0:T(8,128)S(1)}, f32[160,128]{1,0:T(8,128)S(1)}, u32[]{:S(2)}, u32[]{:S(2)}) collective-permute-start(f32[160,128]{1,0:T(8,128)S(1)} %get-tuple-element.30), channel_id=1, source_target_pairs={{0,6},{1,7},{2,4},{3,5},{4,2},{5,3},{6,0},{7,1},{8,14},{9,15},{10,... | collective-permute-start | bytes 245768 | tf_op jit(solution)/shard_map/ppermute | solution.py:111
  18.9 0.5 collective-permute-start.2
  19.4 0.5 collective-permute-start.1
  19.9 2.4 %collective-permute-done.3 = f32[160,128]{1,0:T(8,128)S(1)} collective-permute-done((f32[160,128]{1,0:T(8,128)S(1)}, f32[160,128]{1,0:T(8,128)S(1)}, u32[]{:S(2)}, u32[]{:S(2)}) %collective-permute-start.3) | collective-permute-done | bytes 81952 | tf_op jit(solution)/shard_map/ppermute | solution.py:111
  22.4 1.3 %collective-permute-done.2 = f32[160,128]{1,0:T(8,128)S(1)} collective-permute-done((f32[160,128]{1,0:T(8,128)S(1)}, f32[160,128]{1,0:T(8,128)S(1)}, u32[]{:S(2)}, u32[]{:S(2)}) %collective-permute-start.2) | collective-permute-done | bytes 81952 | tf_op jit(solution)/shard_map/ppermute | solution.py:111
  23.7 0.2 collective-permute-done.1
  23.9 1.6 %collective-permute-start.6 = (f32[160,128]{1,0:T(8,128)S(1)}, f32[160,128]{1,0:T(8,128)S(1)}, u32[]{:S(2)}, u32[]{:S(2)}) collective-permute-start(f32[160,128]{1,0:T(8,128)S(1)} %fusion), channel_id=1, source_target_pairs={{0,24},{1,25},{2,26},{3,27},{4,28},{5,29},{6,30},{7,31},{8,16},{9,... | collective-permute-start | bytes 245768 | tf_op jit(solution)/shard_map/ppermute | solution.py:111
  25.5 1.2 %collective-permute-start.5 = (f32[160,128]{1,0:T(8,128)S(1)}, f32[160,128]{1,0:T(8,128)S(1)}, u32[]{:S(2)}, u32[]{:S(2)}) collective-permute-start(f32[160,128]{1,0:T(8,128)S(1)} %fusion), channel_id=1, source_target_pairs={{0,16},{1,17},{2,18},{3,19},{4,20},{5,21},{6,22},{7,23},{8,24},{9,... | collective-permute-start | bytes 245768 | tf_op jit(solution)/shard_map/ppermute | solution.py:111
  26.8 1.2 %collective-permute-start.4 = (f32[160,128]{1,0:T(8,128)S(1)}, f32[160,128]{1,0:T(8,128)S(1)}, u32[]{:S(2)}, u32[]{:S(2)}) collective-permute-start(f32[160,128]{1,0:T(8,128)S(1)} %fusion), channel_id=1, source_target_pairs={{0,8},{1,9},{2,10},{3,11},{4,12},{5,13},{6,14},{7,15},{8,0},{9,1},... | collective-permute-start | bytes 245768 | tf_op jit(solution)/shard_map/ppermute | solution.py:111
  28.0 3.4 %collective-permute-done.6 = f32[160,128]{1,0:T(8,128)S(1)} collective-permute-done((f32[160,128]{1,0:T(8,128)S(1)}, f32[160,128]{1,0:T(8,128)S(1)}, u32[]{:S(2)}, u32[]{:S(2)}) %collective-permute-start.6) | collective-permute-done | bytes 81952 | tf_op jit(solution)/shard_map/ppermute | solution.py:111
  31.4 0.8 collective-permute-done.5
  32.2 1.0 collective-permute-done.4
  33.2 2.5 %collective-permute-start.9 = (f32[160,128]{1,0:T(8,128)S(1)}, f32[160,128]{1,0:T(8,128)S(1)}, u32[]{:S(2)}, u32[]{:S(2)}) collective-permute-start(f32[160,128]{1,0:T(8,128)S(1)} %add_add_fusion), channel_id=1, source_target_pairs={{0,6},{1,7},{2,4},{3,5},{4,2},{5,3},{6,0},{7,1},{8,14},{9,15},{10,... | collective-permute-start | bytes 245768 | tf_op jit(solution)/shard_map/ppermute | solution.py:111
  35.7 0.7 collective-permute-start.8
  36.4 0.4 collective-permute-start.7
  36.8 2.0 %collective-permute-done.9 = f32[160,128]{1,0:T(8,128)S(1)} collective-permute-done((f32[160,128]{1,0:T(8,128)S(1)}, f32[160,128]{1,0:T(8,128)S(1)}, u32[]{:S(2)}, u32[]{:S(2)}) %collective-permute-start.9) | collective-permute-done | bytes 81952 | tf_op jit(solution)/shard_map/ppermute | solution.py:111
  38.7 1.4 %collective-permute-done.8 = f32[160,128]{1,0:T(8,128)S(1)} collective-permute-done((f32[160,128]{1,0:T(8,128)S(1)}, f32[160,128]{1,0:T(8,128)S(1)}, u32[]{:S(2)}, u32[]{:S(2)}) %collective-permute-start.8) | collective-permute-done | bytes 81952 | tf_op jit(solution)/shard_map/ppermute | solution.py:111
  40.2 0.7 collective-permute-done.7
  40.9 0.1 collective-permute-start.10
  41.0 1.6 %collective-permute-done.10 = f32[640,128]{1,0:T(8,128)S(1)} collective-permute-done((f32[640,128]{1,0:T(8,128)S(1)}, f32[640,128]{1,0:T(8,128)S(1)}, u32[]{:S(2)}, u32[]{:S(2)}) %collective-permute-start.10) | collective-permute-done | bytes 327712 | tf_op jit(solution)/shard_map/ppermute | solution.py:111
  42.7 0.0 copy-done
  42.7 23.3 %iterate.1 = (f32[64,512]{1,0:T(8,128)}, f32[2,32,8,128]{3,2,1,0:T(8,128)S(1)}, f32[2,32,8,128]{3,2,1,0:T(8,128)S(1)}, f32[2,32,8,128]{3,2,1,0:T(8,128)S(1)}, f3...) custom-call(f32[1280,128]{1,0:T(8,128)S(1)} %pad_maximum_fusion.pack, ...), custom_call_target="tpu_custom_call" | custom-call | tf_op jit(solution)/shard_map/iterate/pallas_call | solution.py:266
  66.0 1.4 %collective-permute-start.11 = (f32[2,32,8,128]{3,2,1,0:T(8,128)S(1)}, f32[2,32,8,128]{3,2,1,0:T(8,128)S(1)}, u32[]{:S(2)}, u32[]{:S(2)}) collective-permute-start(f32[2,32,8,128]{3,2,1,0:T(8,128)S(1)} %get-tuple-element.15), channel_id=1, source_target_pairs={{0,4},{1,5},{2,6},{3,7},{4,0},{5,1},{6,2},{7,3},{8,12},{9,13},{10,... | collective-permute-start | bytes 786440 | tf_op jit(solution)/shard_map/ppermute | solution.py:111
  67.4 1.4 %collective-permute-start.13 = (f32[2,32,8,128]{3,2,1,0:T(8,128)S(1)}, f32[2,32,8,128]{3,2,1,0:T(8,128)S(1)}, u32[]{:S(2)}, u32[]{:S(2)}) collective-permute-start(f32[2,32,8,128]{3,2,1,0:T(8,128)S(1)} %get-tuple-element.19), channel_id=1, source_target_pairs={{0,12},{1,13},{2,14},{3,15},{4,8},{5,9},{6,10},{7,11},{8,4},{9,5},... | collective-permute-start | bytes 786440 | tf_op jit(solution)/shard_map/ppermute | solution.py:111
  68.8 1.0 collective-permute-start.14
  69.8 2.6 %collective-permute-start.15 = (f32[2,32,8,128]{3,2,1,0:T(8,128)S(1)}, f32[2,32,8,128]{3,2,1,0:T(8,128)S(1)}, u32[]{:S(2)}, u32[]{:S(2)}) collective-permute-start(f32[2,32,8,128]{3,2,1,0:T(8,128)S(1)} %get-tuple-element.21), channel_id=1, source_target_pairs={{0,20},{1,21},{2,22},{3,23},{4,16},{5,17},{6,18},{7,19},{8,28},{9,... | collective-permute-start | bytes 786440 | tf_op jit(solution)/shard_map/ppermute | solution.py:111
  72.4 1.8 %collective-permute-start.16 = (f32[2,32,8,128]{3,2,1,0:T(8,128)S(1)}, f32[2,32,8,128]{3,2,1,0:T(8,128)S(1)}, u32[]{:S(2)}, u32[]{:S(2)}) collective-permute-start(f32[2,32,8,128]{3,2,1,0:T(8,128)S(1)} %get-tuple-element.22), channel_id=1, source_target_pairs={{0,24},{1,25},{2,26},{3,27},{4,28},{5,29},{6,30},{7,31},{8,16},{9,... | collective-permute-start | bytes 786440 | tf_op jit(solution)/shard_map/ppermute | solution.py:111
  74.2 5.8 %collective-permute-done.11.refs_1_ = f32[2,32,8,128]{3,2,1,0:T(8,128)S(1)} collective-permute-done((f32[2,32,8,128]{3,2,1,0:T(8,128)S(1)}, f32[2,32,8,128]{3,2,1,0:T(8,128)S(1)}, u32[]{:S(2)}, u32[]{:S(2)}) %collective-permute-start.11) | collective-permute-done | bytes 262176 | tf_op jit(solution)/shard_map/ppermute | solution.py:111
  80.0 1.4 %collective-permute-start.17 = (f32[2,32,8,128]{3,2,1,0:T(8,128)S(1)}, f32[2,32,8,128]{3,2,1,0:T(8,128)S(1)}, u32[]{:S(2)}, u32[]{:S(2)}) collective-permute-start(f32[2,32,8,128]{3,2,1,0:T(8,128)S(1)} %get-tuple-element.23), channel_id=1, source_target_pairs={{0,28},{1,29},{2,30},{3,31},{4,24},{5,25},{6,26},{7,27},{8,20},{9,... | collective-permute-start | bytes 786440 | tf_op jit(solution)/shard_map/ppermute | solution.py:111
  81.5 0.0 collective-permute-done.13.refs_3_
  81.5 0.7 collective-permute-start.12
  82.2 16.7 %collective-permute-done.14.refs_4_ = f32[2,32,8,128]{3,2,1,0:T(8,128)S(1)} collective-permute-done((f32[2,32,8,128]{3,2,1,0:T(8,128)S(1)}, f32[2,32,8,128]{3,2,1,0:T(8,128)S(1)}, u32[]{:S(2)}, u32[]{:S(2)}) %collective-permute-start.14) | collective-permute-done | bytes 262176 | tf_op jit(solution)/shard_map/ppermute | solution.py:111
  98.9 5.8 %collective-permute-done.15.refs_5_ = f32[2,32,8,128]{3,2,1,0:T(8,128)S(1)} collective-permute-done((f32[2,32,8,128]{3,2,1,0:T(8,128)S(1)}, f32[2,32,8,128]{3,2,1,0:T(8,128)S(1)}, u32[]{:S(2)}, u32[]{:S(2)}) %collective-permute-start.15) | collective-permute-done | bytes 262176 | tf_op jit(solution)/shard_map/ppermute | solution.py:111
  104.7 7.3 %collective-permute-done.16.refs_6_ = f32[2,32,8,128]{3,2,1,0:T(8,128)S(1)} collective-permute-done((f32[2,32,8,128]{3,2,1,0:T(8,128)S(1)}, f32[2,32,8,128]{3,2,1,0:T(8,128)S(1)}, u32[]{:S(2)}, u32[]{:S(2)}) %collective-permute-start.16) | collective-permute-done | bytes 262176 | tf_op jit(solution)/shard_map/ppermute | solution.py:111
  112.0 5.0 %collective-permute-done.17.refs_7_ = f32[2,32,8,128]{3,2,1,0:T(8,128)S(1)} collective-permute-done((f32[2,32,8,128]{3,2,1,0:T(8,128)S(1)}, f32[2,32,8,128]{3,2,1,0:T(8,128)S(1)}, u32[]{:S(2)}, u32[]{:S(2)}) %collective-permute-start.17) | collective-permute-done | bytes 262176 | tf_op jit(solution)/shard_map/ppermute | solution.py:111
  117.0 0.0 collective-permute-done.12.refs_2_
  117.0 1.7 %turn.1 = f32[256,8,256]{2,1,0:T(8,128)} custom-call(f32[2,32,8,128]{3,2,1,0:T(8,128)S(1)} %get-tuple-element.14.refs_0_, f32[2,32,8,128]{3,2,1,0:T(8,128)S(1)} %collective-permute-done.11.refs_1_, f32[2,32,8,128]{3,2,1,0:T(8,128)S(1)} %collective-permute-done.12.refs_2_, f32[2,32,8,128]{3,2,1,0:T(8,128)S(1)} %collective-permute-done.13.refs_3_, ...), custom_call_target="tpu_custom_call" | custom-call | tf_op jit(solution)/shard_map/turn/pallas_call | solution.py:328
  (9 shorter events, 0.3 us)
Async XLA Ops:
  0.6 42.1 %copy-start = (f32[512,64]{0,1:T(8,128)S(1)}, f32[512,64]{0,1:T(8,128)}, u32[]{:S(2)}) copy-start(f32[512,64]{0,1:T(8,128)} %param.3) | copy-start | bytes 393220
  14.6 1.7 %collective-permute-start = (f32[640,128]{1,0:T(8,128)S(1)}, f32[640,128]{1,0:T(8,128)S(1)}, u32[]{:S(2)}, u32[]{:S(2)}) collective-permute-start(f32[640,128]{1,0:T(8,128)S(1)} %dynamic-slice_bitcast_fusion), channel_id=1, source_target_pairs={{0,1},{1,0},{2,3},{3,2},{4,5},{5,4},{6,7},{7,6},{8,9},{9,8},{10,11... | collective-permute-start | bytes 983048 | tf_op jit(solution)/shard_map/ppermute | solution.py:111
  16.4 6.0 %collective-permute-start.3 = (f32[160,128]{1,0:T(8,128)S(1)}, f32[160,128]{1,0:T(8,128)S(1)}, u32[]{:S(2)}, u32[]{:S(2)}) collective-permute-start(f32[160,128]{1,0:T(8,128)S(1)} %get-tuple-element.30), channel_id=1, source_target_pairs={{0,6},{1,7},{2,4},{3,5},{4,2},{5,3},{6,0},{7,1},{8,14},{9,15},{10,... | collective-permute-start | bytes 245768 | tf_op jit(solution)/shard_map/ppermute | solution.py:111
  18.9 4.8 %collective-permute-start.2 = (f32[160,128]{1,0:T(8,128)S(1)}, f32[160,128]{1,0:T(8,128)S(1)}, u32[]{:S(2)}, u32[]{:S(2)}) collective-permute-start(f32[160,128]{1,0:T(8,128)S(1)} %get-tuple-element.31), channel_id=1, source_target_pairs={{0,4},{1,5},{2,6},{3,7},{4,0},{5,1},{6,2},{7,3},{8,12},{9,13},{10,... | collective-permute-start | bytes 245768 | tf_op jit(solution)/shard_map/ppermute | solution.py:111
  19.4 4.4 %collective-permute-start.1 = (f32[160,128]{1,0:T(8,128)S(1)}, f32[160,128]{1,0:T(8,128)S(1)}, u32[]{:S(2)}, u32[]{:S(2)}) collective-permute-start(f32[160,128]{1,0:T(8,128)S(1)} %get-tuple-element.32), channel_id=1, source_target_pairs={{0,2},{1,3},{2,0},{3,1},{4,6},{5,7},{6,4},{7,5},{8,10},{9,11},{10,... | collective-permute-start | bytes 245768 | tf_op jit(solution)/shard_map/ppermute | solution.py:111
  23.9 7.5 %collective-permute-start.6 = (f32[160,128]{1,0:T(8,128)S(1)}, f32[160,128]{1,0:T(8,128)S(1)}, u32[]{:S(2)}, u32[]{:S(2)}) collective-permute-start(f32[160,128]{1,0:T(8,128)S(1)} %fusion), channel_id=1, source_target_pairs={{0,24},{1,25},{2,26},{3,27},{4,28},{5,29},{6,30},{7,31},{8,16},{9,... | collective-permute-start | bytes 245768 | tf_op jit(solution)/shard_map/ppermute | solution.py:111
  25.5 6.7 %collective-permute-start.5 = (f32[160,128]{1,0:T(8,128)S(1)}, f32[160,128]{1,0:T(8,128)S(1)}, u32[]{:S(2)}, u32[]{:S(2)}) collective-permute-start(f32[160,128]{1,0:T(8,128)S(1)} %fusion), channel_id=1, source_target_pairs={{0,16},{1,17},{2,18},{3,19},{4,20},{5,21},{6,22},{7,23},{8,24},{9,... | collective-permute-start | bytes 245768 | tf_op jit(solution)/shard_map/ppermute | solution.py:111
  26.8 6.4 %collective-permute-start.4 = (f32[160,128]{1,0:T(8,128)S(1)}, f32[160,128]{1,0:T(8,128)S(1)}, u32[]{:S(2)}, u32[]{:S(2)}) collective-permute-start(f32[160,128]{1,0:T(8,128)S(1)} %fusion), channel_id=1, source_target_pairs={{0,8},{1,9},{2,10},{3,11},{4,12},{5,13},{6,14},{7,15},{8,0},{9,1},... | collective-permute-start | bytes 245768 | tf_op jit(solution)/shard_map/ppermute | solution.py:111
  33.2 5.5 %collective-permute-start.9 = (f32[160,128]{1,0:T(8,128)S(1)}, f32[160,128]{1,0:T(8,128)S(1)}, u32[]{:S(2)}, u32[]{:S(2)}) collective-permute-start(f32[160,128]{1,0:T(8,128)S(1)} %add_add_fusion), channel_id=1, source_target_pairs={{0,6},{1,7},{2,4},{3,5},{4,2},{5,3},{6,0},{7,1},{8,14},{9,15},{10,... | collective-permute-start | bytes 245768 | tf_op jit(solution)/shard_map/ppermute | solution.py:111
  35.7 4.4 %collective-permute-start.8 = (f32[160,128]{1,0:T(8,128)S(1)}, f32[160,128]{1,0:T(8,128)S(1)}, u32[]{:S(2)}, u32[]{:S(2)}) collective-permute-start(f32[160,128]{1,0:T(8,128)S(1)} %add_add_fusion), channel_id=1, source_target_pairs={{0,4},{1,5},{2,6},{3,7},{4,0},{5,1},{6,2},{7,3},{8,12},{9,13},{10,... | collective-permute-start | bytes 245768 | tf_op jit(solution)/shard_map/ppermute | solution.py:111
  36.4 4.4 %collective-permute-start.7 = (f32[160,128]{1,0:T(8,128)S(1)}, f32[160,128]{1,0:T(8,128)S(1)}, u32[]{:S(2)}, u32[]{:S(2)}) collective-permute-start(f32[160,128]{1,0:T(8,128)S(1)} %add_add_fusion), channel_id=1, source_target_pairs={{0,2},{1,3},{2,0},{3,1},{4,6},{5,7},{6,4},{7,5},{8,10},{9,11},{10,... | collective-permute-start | bytes 245768 | tf_op jit(solution)/shard_map/ppermute | solution.py:111
  40.9 1.7 %collective-permute-start.10 = (f32[640,128]{1,0:T(8,128)S(1)}, f32[640,128]{1,0:T(8,128)S(1)}, u32[]{:S(2)}, u32[]{:S(2)}) collective-permute-start(f32[640,128]{1,0:T(8,128)S(1)} %pad_maximum_fusion.1), channel_id=1, source_target_pairs={{0,1},{1,0},{2,3},{3,2},{4,5},{5,4},{6,7},{7,6},{8,9},{9,8},{10,11... | collective-permute-start | bytes 983048 | tf_op jit(solution)/shard_map/ppermute | solution.py:111
  66.0 14.0 %collective-permute-start.11 = (f32[2,32,8,128]{3,2,1,0:T(8,128)S(1)}, f32[2,32,8,128]{3,2,1,0:T(8,128)S(1)}, u32[]{:S(2)}, u32[]{:S(2)}) collective-permute-start(f32[2,32,8,128]{3,2,1,0:T(8,128)S(1)} %get-tuple-element.15), channel_id=1, source_target_pairs={{0,4},{1,5},{2,6},{3,7},{4,0},{5,1},{6,2},{7,3},{8,12},{9,13},{10,... | collective-permute-start | bytes 786440 | tf_op jit(solution)/shard_map/ppermute | solution.py:111
  67.4 14.0 %collective-permute-start.13 = (f32[2,32,8,128]{3,2,1,0:T(8,128)S(1)}, f32[2,32,8,128]{3,2,1,0:T(8,128)S(1)}, u32[]{:S(2)}, u32[]{:S(2)}) collective-permute-start(f32[2,32,8,128]{3,2,1,0:T(8,128)S(1)} %get-tuple-element.19), channel_id=1, source_target_pairs={{0,12},{1,13},{2,14},{3,15},{4,8},{5,9},{6,10},{7,11},{8,4},{9,5},... | collective-permute-start | bytes 786440 | tf_op jit(solution)/shard_map/ppermute | solution.py:111
  68.8 30.1 %collective-permute-start.14 = (f32[2,32,8,128]{3,2,1,0:T(8,128)S(1)}, f32[2,32,8,128]{3,2,1,0:T(8,128)S(1)}, u32[]{:S(2)}, u32[]{:S(2)}) collective-permute-start(f32[2,32,8,128]{3,2,1,0:T(8,128)S(1)} %get-tuple-element.20), channel_id=1, source_target_pairs={{0,16},{1,17},{2,18},{3,19},{4,20},{5,21},{6,22},{7,23},{8,24},{9,... | collective-permute-start | bytes 786440 | tf_op jit(solution)/shard_map/ppermute | solution.py:111
  69.8 34.8 %collective-permute-start.15 = (f32[2,32,8,128]{3,2,1,0:T(8,128)S(1)}, f32[2,32,8,128]{3,2,1,0:T(8,128)S(1)}, u32[]{:S(2)}, u32[]{:S(2)}) collective-permute-start(f32[2,32,8,128]{3,2,1,0:T(8,128)S(1)} %get-tuple-element.21), channel_id=1, source_target_pairs={{0,20},{1,21},{2,22},{3,23},{4,16},{5,17},{6,18},{7,19},{8,28},{9,... | collective-permute-start | bytes 786440 | tf_op jit(solution)/shard_map/ppermute | solution.py:111
  72.4 39.6 %collective-permute-start.16 = (f32[2,32,8,128]{3,2,1,0:T(8,128)S(1)}, f32[2,32,8,128]{3,2,1,0:T(8,128)S(1)}, u32[]{:S(2)}, u32[]{:S(2)}) collective-permute-start(f32[2,32,8,128]{3,2,1,0:T(8,128)S(1)} %get-tuple-element.22), channel_id=1, source_target_pairs={{0,24},{1,25},{2,26},{3,27},{4,28},{5,29},{6,30},{7,31},{8,16},{9,... | collective-permute-start | bytes 786440 | tf_op jit(solution)/shard_map/ppermute | solution.py:111
  80.0 37.0 %collective-permute-start.17 = (f32[2,32,8,128]{3,2,1,0:T(8,128)S(1)}, f32[2,32,8,128]{3,2,1,0:T(8,128)S(1)}, u32[]{:S(2)}, u32[]{:S(2)}) collective-permute-start(f32[2,32,8,128]{3,2,1,0:T(8,128)S(1)} %get-tuple-element.23), channel_id=1, source_target_pairs={{0,28},{1,29},{2,30},{3,31},{4,24},{5,25},{6,26},{7,27},{8,20},{9,... | collective-permute-start | bytes 786440 | tf_op jit(solution)/shard_map/ppermute | solution.py:111
  81.5 35.6 %collective-permute-start.12 = (f32[2,32,8,128]{3,2,1,0:T(8,128)S(1)}, f32[2,32,8,128]{3,2,1,0:T(8,128)S(1)}, u32[]{:S(2)}, u32[]{:S(2)}) collective-permute-start(f32[2,32,8,128]{3,2,1,0:T(8,128)S(1)} %get-tuple-element.18), channel_id=1, source_target_pairs={{0,8},{1,9},{2,10},{3,11},{4,12},{5,13},{6,14},{7,15},{8,0},{9,1},... | collective-permute-start | bytes 786440 | tf_op jit(solution)/shard_map/ppermute | solution.py:111
